TPU v7x, 128 devices: a whole 4x4x4 slice. The times are simulated.
128 devices in a mesh: row: 8 (over x, core), col: 16 (over z, y).
Axes of the slice: x: 4, y: 4, z: 4, core: 2. Of those that a mesh axis runs over, the one named last changes fastest.
Arguments:
- reflectance: bfloat16 [4, 65536, 128], P(None, ('row', 'col')), may hold values from 0.049804688 to 0.59765625
- kernel_id: int32 [65536], P(('row', 'col')), may hold values from 0 to 7
- dest_device: int32 [65536, 1], P(('row', 'col')), may hold values from 0 to 127; in each aligned block of 512 rows (0 to 511, 512 to 1023, ...) at most 8 rows name the same one
- dest_block: int32 [65536], P(('row', 'col')), may hold values from 0 to 511
- regrid_weight: bfloat16 [8, 128, 128], replicated, may hold values from 0 to 0.82, as said below
- depth0: float32 [512, 16384], P('row', 'col'), may hold values from 0.01 to 3, as said below
- terrain: float32 [512, 16384], P('row', 'col'), may hold values from -0.6 to 0.6
- rain: float32 [512, 16384], P('row', 'col'), may hold values from 0.01 to 0.1
- burn_mask: int32 [512, 16384], P('row', 'col'), may hold values 0 or 1
- land_class: int32 [512, 16384], P('row', 'col'), may hold values from 0 to 15
- infil_table: float32 [16], replicated, may hold values from 0.01 to 0.1
- rough_table: float32 [16], replicated, may hold values from 0.02 to 0.2
Outputs:
- depth: float32 [512, 16384], P('row', 'col')
- east_flow: float32 [512, 16384], P('row', 'col')
- north_flow: float32 [512, 16384], P('row', 'col')
Inputs may be any that keep to these rules, and one draw needn't show every extreme that they name: `dest_device`: the sensor blocks of one device name each destination device at most 8 times, a bound that some block reaches. `regrid_weight`: Nonnegative; the diagonal of each block exceeds 0.4. `depth0`: the largest depth differs from draw to draw.
All inputs are finite; a program needn't handle non-finite values. No bound on the sum of `burn_mask` on one device may be relied on, other than what follows from the above.
Results may differ from a plain program's by a relative error of at most 0.0003.
Values sent between devices are 32-bit elements; how exact they have to be, the bound alone decides.
A program may use at most 64 MiB of HBM per device.

v0:
```python
import jax
import jax.numpy as jnp
from jax import lax
from jax.sharding import PartitionSpec as P

ITERS = 6


GRAVITY = 9.81
CELL_SIZE = 10.0
COURANT = 0.4
DEPTH_FLOOR = 0.05
BURN_LOSS = 1.5
BURN_SMOOTH = 0.5


def with_halo(value, sides, width):
    for axis, dim in sides:
        peers, length = (lax.axis_size(axis), value.shape[dim])
        up = [(i, (i + 1) % peers) for i in range(peers - 1)]
        down = [(j, i) for i, j in up]
        last = lax.slice_in_dim(value, length - width, length, axis=dim)
        initial = lax.slice_in_dim(value, 0, width, axis=dim)
        before = lax.ppermute(last, axis, up)
        after = lax.ppermute(initial, axis, down)
        value = jnp.concatenate([before, value, after], axis=dim)
    return value


def ratio(nir, swir):
    return (nir - swir) / (nir + swir)


def lookup(table, classes):
    result = jnp.zeros(classes.shape, jnp.float32)
    for entry in range(table.shape[0]):
        result = result + jnp.where(classes == entry, table[entry], jnp.float32(0.0))
    return result


def wave_speed(state):
    floored = jnp.maximum(state[0], DEPTH_FLOOR)
    celerity = jnp.sqrt(GRAVITY * jnp.maximum(state[0], 0.0))
    return jnp.maximum(jnp.abs(state[1] / floored), jnp.abs(state[2] / floored)) + celerity


def top_speed(state):
    return lax.pmax(jnp.max(wave_speed(state)), ("row", "col"))


def advance(padded, relief, roughness, capacity_in, rainfall, time_step):
    depth = padded[0]
    east = padded[1]
    north = padded[2]
    floored = jnp.maximum(depth, DEPTH_FLOOR)
    east_speed = east / floored
    north_speed = north / floored
    celerity = jnp.sqrt(GRAVITY * jnp.maximum(depth, 0.0))
    pressure = 0.5 * GRAVITY * depth * depth
    flux_east = jnp.stack([east, east * east_speed + pressure, east * north_speed])
    flux_north = jnp.stack([north, north * east_speed, north * north_speed + pressure])
    reach_east = jnp.abs(east_speed) + celerity
    reach_north = jnp.abs(north_speed) + celerity
    face_reach = jnp.maximum(reach_east[:, :-1], reach_east[:, 1:])
    face_east = 0.5 * (flux_east[:, :, :-1] + flux_east[:, :, 1:]) - 0.5 * face_reach * (
        padded[:, :, 1:] - padded[:, :, :-1]
    )
    row_reach = jnp.maximum(reach_north[:-1], reach_north[1:])
    face_north = 0.5 * (flux_north[:, :-1] + flux_north[:, 1:]) - 0.5 * row_reach * (
        padded[:, 1:] - padded[:, :-1]
    )
    change = (
        face_east[:, 1:-1, 1:]
        - face_east[:, 1:-1, :-1]
        + face_north[:, 1:, 1:-1]
        - face_north[:, :-1, 1:-1]
    ) / CELL_SIZE
    old = padded[:, 1:-1, 1:-1]
    old_depth = depth[1:-1, 1:-1]
    slope_east = (relief[1:-1, 2:] - relief[1:-1, :-2]) / (2.0 * CELL_SIZE)
    slope_north = (relief[2:, 1:-1] - relief[:-2, 1:-1]) / (2.0 * CELL_SIZE)
    wetted = old[0] - time_step * change[0] + time_step * rainfall
    wetted = wetted - jnp.minimum(time_step * capacity_in, wetted)
    moved_east = old[1] - time_step * change[1] - time_step * GRAVITY * old_depth * slope_east
    moved_north = old[2] - time_step * change[2] - time_step * GRAVITY * old_depth * slope_north
    inner_floor = floored[1:-1, 1:-1]
    magnitude = jnp.sqrt(east_speed[1:-1, 1:-1] ** 2 + north_speed[1:-1, 1:-1] ** 2)
    drag = 1.0 + time_step * GRAVITY * roughness * roughness * magnitude / inner_floor ** (
        4.0 / 3.0
    )
    return jnp.stack([wetted, moved_east / drag, moved_north / drag])


def body(
    reflectance,
    kernel_id,
    dest_device,
    dest_block,
    regrid_weight,
    depth0,
    terrain,
    rain,
    burn_mask,
    land_class,
    infil_table,
    rough_table,
):
    tile_rows, tile_cols = depth0.shape
    blocks_here = reflectance.shape[1]
    width = reflectance.shape[2]
    row_count = lax.axis_size("row")
    col_count = lax.axis_size("col")
    device_count = row_count * col_count
    capacity = 2 * blocks_here // device_count
    kernels = regrid_weight.shape[0]
    bands = reflectance.astype(jnp.float32)
    burn_index = (ratio(bands[0], bands[1]) - ratio(bands[2], bands[3])).astype(jnp.bfloat16)
    stacked_weight = regrid_weight.transpose(1, 0, 2).reshape(width, kernels * width)
    every_kernel = jnp.dot(burn_index, stacked_weight, preferred_element_type=jnp.float32).reshape(
        blocks_here, kernels, width
    )
    picked = kernel_id[:, None] == jnp.arange(kernels, dtype=jnp.int32)[None, :]
    regridded = jnp.sum(jnp.where(picked[:, :, None], every_kernel, jnp.float32(0.0)), axis=1)
    target = dest_device[:, 0]
    member = (target[:, None] == jnp.arange(device_count, dtype=jnp.int32)[None, :]).astype(
        jnp.int32
    )
    ranks = jnp.sum(jnp.cumsum(member, axis=0) * member, axis=1) - 1
    position = target * capacity + ranks
    outgoing = jnp.zeros((device_count * capacity, width), jnp.float32).at[position].set(regridded)
    labels = (
        jnp.full((device_count * capacity,), blocks_here, jnp.int32).at[position].set(dest_block)
    )
    incoming, arrived = (
        lax.all_to_all(
            outgoing.reshape(device_count, capacity, width),
            ("row", "col"),
            split_axis=0,
            concat_axis=0,
            tiled=True,
        ),
        lax.all_to_all(
            labels.reshape(device_count, capacity),
            ("row", "col"),
            split_axis=0,
            concat_axis=0,
            tiled=True,
        ),
    )
    severity = (
        jnp.zeros((blocks_here, width), jnp.float32)
        .at[arrived.reshape(-1)]
        .add(incoming.reshape(-1, width), mode="drop")
    )
    severity = severity.reshape(tile_rows, tile_cols)
    burned = burn_mask.astype(jnp.float32)
    infiltration = lookup(infil_table, land_class) * jnp.exp(
        -BURN_LOSS * burned * jnp.maximum(severity, 0.0)
    )
    roughness = lookup(rough_table, land_class) * (1.0 - BURN_SMOOTH * burned)
    zeros_field = jnp.zeros(depth0.shape, jnp.float32)
    state = jnp.stack([depth0, zeros_field, zeros_field])
    relief = with_halo(terrain, (("row", 0), ("col", 1)), 1)
    for iteration in range(ITERS):
        time_step = COURANT * CELL_SIZE / top_speed(state)
        padded = with_halo(state, (("row", 1), ("col", 2)), 1)
        state = advance(padded, relief, roughness, infiltration, rain, time_step)
    return (state[0], state[1], state[2])


def solution(mesh):
    return jax.shard_map(
        body,
        mesh=mesh,
        in_specs=(
            P(None, ("row", "col"), None),
            P(("row", "col")),
            P(("row", "col"), None),
            P(("row", "col")),
            P(),
            P("row", "col"),
            P("row", "col"),
            P("row", "col"),
            P("row", "col"),
            P("row", "col"),
            P(),
            P(),
        ),
        out_specs=(P("row", "col"), P("row", "col"), P("row", "col")),
        check_vma=False,
    )
```

profile of v0, /device:TPU:1, one launch (start us, length us, event | category | flops | bytes accessed | tf_op | source)
XLA Modules:
  0.0 597.2 jit_solution(2013693838649214944)
XLA Ops:
  1.4 4.6 collective-permute-start
  6.1 1.9 collective-permute-start.1
  8.8 3.6 collective-permute-start.4
  12.5 1.9 collective-permute-start.5
  15.8 2.6 scatter_custom_fusion
  19.1 10.6 %all-to-all-start = ((s32[128,1,8]{2,1,0:T(1,128)}), s32[128,1,8]{2,1,0:T(1,128)S(1)}, u32[]{:S(2)}, u32[]{:S(2)}) async-start(s32[128,1,8]{2,1,0:T(1,128)} %bitcast.28), calls=%async_computation | async-start | bytes 131072 | tf_op jit(solution)/shard_map/all_to_all | solution.py:142
  30.5 1.4 broadcast_compare_fusion.15
  34.8 67.2 %pmax.42 = f32[]{:T(128)} all-reduce(f32[]{:T(128)} %add_reduce_fusion.5), channel_id=1, replica_groups=mesh['row'=8,'col'=16] {'row','col'}, use_global_device_ids=true, to_apply=%region_1.2 | all-reduce | flops 1 | bytes 8 | tf_op jit(solution)/shard_map/pmax | solution.py:48
  102.1 2.5 scatter_custom_fusion.1
  105.3 5.4 all-to-all-start.1
  112.4 3.4 collective-permute-start.2
  115.7 1.3 collective-permute-start.3
  117.7 1.3 collective-permute-start.6
  119.0 4.8 collective-permute-start.7
  123.8 0.9 concatenate.89
  125.6 1.0 abs_add_fusion.11
  128.8 6.1 %scatter_custom_fusion.2 = f32[512,128]{1,0:T(8,128)S(1)} fusion(s32[1024]{0:T(1024)S(1)} %bitcast.390, f32[128,8,128]{2,1,0:T(8,128)} %all-to-all-done.1, f32[]{:T(128)} %constant.31.clone.1), kind=kCustom, calls=%fused_computation.106 | custom fusion | flops 131072 | bytes 786436 | tf_op jit(solution)/shard_map/scatter-add | solution.py:153
  135.0 24.2 %add_reduce_fusion.4 = (f32[]{:T(128)}, f32[64,1024]{1,0:T(8,128)S(1)}, f32[64,1024]{1,0:T(8,128)S(1)}, f32[64,1024]{1,0:T(8,128)S(1)}, f32[64,1024]{1,0:T(8,128...) fusion(f32[1,1024]{1,0:T(1,128)S(1)} %collective-permute-done.5, f32[64,1024]{1,0:T(8,128)S(1)} %copy-done, ...), kind=kLoop, calls=%fused_computation.353 | loop fusion | flops 7602175 | bytes 5777556 | tf_op jit(solution)/shard_map/reduce_max | solution.py:48
  159.3 4.2 collective-permute-start.8
  163.5 1.9 collective-permute-start.9
  165.4 3.1 collective-permute-done.9
  168.6 0.9 copy-done.6
  169.7 3.6 collective-permute-start.10
  173.3 1.3 collective-permute-start.11
  174.6 70.1 %pmax.43 = f32[]{:T(128)} all-reduce(f32[]{:T(128)} %get-tuple-element.41), channel_id=1, replica_groups=mesh['row'=8,'col'=16] {'row','col'}, use_global_device_ids=true, to_apply=%region_10.11 | all-reduce | flops 1 | bytes 8 | tf_op jit(solution)/shard_map/pmax | solution.py:48
  245.4 1.6 concatenate.98
  249.6 1.6 add_reduce_fusion.3
  251.3 3.8 collective-permute-start.12
  255.1 1.9 collective-permute-start.13
  257.1 3.1 collective-permute-done.13
  260.3 0.9 copy-done.3
  261.3 1.6 collective-permute-start.14
  262.9 1.3 collective-permute-start.15
  264.2 66.8 %pmax.44 = f32[]{:T(128)} all-reduce(f32[]{:T(128)} %get-tuple-element.32), channel_id=1, replica_groups=mesh['row'=8,'col'=16] {'row','col'}, use_global_device_ids=true, to_apply=%region_12.13 | all-reduce | flops 1 | bytes 8 | tf_op jit(solution)/shard_map/pmax | solution.py:48
  331.7 1.6 concatenate.102
  335.8 1.6 add_reduce_fusion.2
  337.6 3.4 collective-permute-start.16
  341.0 1.9 collective-permute-start.17
  342.9 3.1 collective-permute-done.17
  346.1 0.9 copy-done.4
  347.1 1.5 collective-permute-start.18
  348.7 1.3 collective-permute-start.19
  350.0 67.1 %pmax.45 = f32[]{:T(128)} all-reduce(f32[]{:T(128)} %get-tuple-element.23), channel_id=1, replica_groups=mesh['row'=8,'col'=16] {'row','col'}, use_global_device_ids=true, to_apply=%region_14.15 | all-reduce | flops 1 | bytes 8 | tf_op jit(solution)/shard_map/pmax | solution.py:48
  417.8 1.6 concatenate.106
  421.9 1.6 add_reduce_fusion.1
  423.7 3.4 collective-permute-start.20
  427.1 1.9 collective-permute-start.21
  429.0 3.1 collective-permute-done.21
  432.2 0.9 copy-done.5
  433.2 2.1 collective-permute-start.22
  435.3 1.3 collective-permute-start.23
  436.6 66.5 %pmax.46 = f32[]{:T(128)} all-reduce(f32[]{:T(128)} %get-tuple-element.14), channel_id=1, replica_groups=mesh['row'=8,'col'=16] {'row','col'}, use_global_device_ids=true, to_apply=%region_16.17 | all-reduce | flops 1 | bytes 8 | tf_op jit(solution)/shard_map/pmax | solution.py:48
  503.8 1.6 concatenate.110
  508.0 1.6 add_reduce_fusion
  509.7 3.2 collective-permute-start.24
  512.9 1.9 collective-permute-start.25
  514.9 3.1 collective-permute-done.25
  518.0 0.9 copy-done.2
  519.1 2.1 collective-permute-start.26
  521.2 1.3 collective-permute-start.27
  522.5 66.8 %pmax.47 = f32[]{:T(128)} all-reduce(f32[]{:T(128)} %get-tuple-element.5), channel_id=1, replica_groups=mesh['row'=8,'col'=16] {'row','col'}, use_global_device_ids=true, to_apply=%region_18.19 | all-reduce | flops 1 | bytes 8 | tf_op jit(solution)/shard_map/pmax | solution.py:48
  590.0 1.6 concatenate.114
  594.2 1.4 fusion.77
  595.6 1.1 fusion.83
  (161 shorter events, 26.7 us)
Async XLA Ops:
  0.6 14.9 %copy-start.17 = (s32[512,1]{0,1:T(1,128)S(1)}, s32[512,1]{0,1:T(1,128)}, u32[]{:S(2)}) copy-start(s32[512,1]{0,1:T(1,128)} %param.14) | copy-start | bytes 6148
  1.4 28.3 %copy-start.7 = (f32[64,1024]{1,0:T(8,128)S(1)}, f32[64,1024]{1,0:T(8,128)}, u32[]{:S(2)}) copy-start(f32[64,1024]{1,0:T(8,128)} %param.17) | copy-start | bytes 786436
  1.4 110.7 %collective-permute-start = (f32[3,1,1024]{2,1,0:T(1,128)S(1)}, f32[3,1,1024]{2,1,0:T(1,128)S(1)}, u32[]{:S(2)}, u32[]{:S(2)}) collective-permute-start(f32[3,1,1024]{2,1,0:T(1,128)S(1)} %get-tuple-element.174), channel_id=1, source_target_pairs={{0,16},{16,32},{32,48},{48,64},{64,80},{80,96},{96,112},{1,17},{17... | collective-permute-start | bytes 36872 | tf_op jit(solution)/shard_map/ppermute | solution.py:24
  6.1 106.0 %collective-permute-start.1 = (f32[3,1,1024]{2,1,0:T(1,128)S(1)}, f32[3,1,1024]{2,1,0:T(1,128)S(1)}, u32[]{:S(2)}, u32[]{:S(2)}) collective-permute-start(f32[3,1,1024]{2,1,0:T(1,128)S(1)} %get-tuple-element.175), channel_id=1, source_target_pairs={{16,0},{32,16},{48,32},{64,48},{80,64},{96,80},{112,96},{17,1},{33... | collective-permute-start | bytes 36872 | tf_op jit(solution)/shard_map/ppermute | solution.py:25
  8.8 108.2 %collective-permute-start.4 = (f32[1,1024]{1,0:T(1,128)S(1)}, f32[1,1024]{1,0:T(1,128)S(1)}, u32[]{:S(2)}, u32[]{:S(2)}) collective-permute-start(f32[1,1024]{1,0:T(1,128)S(1)} %get-tuple-element.176), channel_id=1, source_target_pairs={{0,16},{16,32},{32,48},{48,64},{64,80},{80,96},{96,112},{1,17},{17... | collective-permute-start | bytes 12296 | tf_op jit(solution)/shard_map/ppermute | solution.py:24
  12.5 104.6 %collective-permute-start.5 = (f32[1,1024]{1,0:T(1,128)S(1)}, f32[1,1024]{1,0:T(1,128)S(1)}, u32[]{:S(2)}, u32[]{:S(2)}) collective-permute-start(f32[1,1024]{1,0:T(1,128)S(1)} %get-tuple-element.177), channel_id=1, source_target_pairs={{16,0},{32,16},{48,32},{64,48},{80,64},{96,80},{112,96},{17,1},{33... | collective-permute-start | bytes 12296 | tf_op jit(solution)/shard_map/ppermute | solution.py:25
  15.2 15.3 %copy-start.13 = (s32[64,1024]{1,0:T(8,128)S(1)}, s32[64,1024]{1,0:T(8,128)}, u32[]{:S(2)}) copy-start(s32[64,1024]{1,0:T(8,128)} %param.21) | copy-start | bytes 786436
  15.5 16.4 %copy-start.15 = (f32[16]{0:T(128)S(1)}, f32[16]{0:T(128)}, u32[]{:S(2)}) copy-start(f32[16]{0:T(128)} %param.22) | copy-start | bytes 196
  15.5 17.1 %copy-start.10 = (bf16[4,512,128]{2,1,0:T(8,128)(2,1)S(1)}, bf16[4,512,128]{2,1,0:T(8,128)(2,1)}, u32[]{:S(2)}) copy-start(bf16[4,512,128]{2,1,0:T(8,128)(2,1)} %param.12) | copy-start | bytes 1572868
  19.1 86.2 %all-to-all-start = ((s32[128,1,8]{2,1,0:T(1,128)}), s32[128,1,8]{2,1,0:T(1,128)S(1)}, u32[]{:S(2)}, u32[]{:S(2)}) async-start(s32[128,1,8]{2,1,0:T(1,128)} %bitcast.28), calls=%async_computation | async-start | bytes 131072 | tf_op jit(solution)/shard_map/all_to_all | solution.py:142
  31.9 1.0 copy-start.14
  32.6 0.7 copy-start.18
  33.3 0.8 copy-start.16
  105.3 23.5 %all-to-all-start.1 = ((f32[128,8,128]{2,1,0:T(8,128)}), f32[128,8,128]{2,1,0:T(8,128)}, u32[]{:S(2)}, u32[]{:S(2)}) async-start(f32[128,8,128]{2,1,0:T(8,128)} %bitcast.36), calls=%async_computation.1 | async-start | bytes 1048576 | tf_op jit(solution)/shard_map/all_to_all | solution.py:135
  112.1 4.9 copy-start
  112.4 11.5 %collective-permute-start.2 = (f32[3,66,1]{2,1,0:T(8,128)S(1)}, f32[3,66,1]{2,1,0:T(8,128)S(1)}, u32[]{:S(2)}, u32[]{:S(2)}) collective-permute-start(f32[3,66,1]{2,1,0:T(8,128)S(1)} %get-tuple-element.133), channel_id=1, source_target_pairs={{0,1},{1,2},{2,3},{3,4},{4,5},{5,6},{6,7},{7,8},{8,9},{9,10},{10,1... | collective-permute-start | bytes 2384 | tf_op jit(solution)/shard_map/ppermute | solution.py:24
  115.7 8.1 %collective-permute-start.3 = (f32[3,66,1]{2,1,0:T(8,128)S(1)}, f32[3,66,1]{2,1,0:T(8,128)S(1)}, u32[]{:S(2)}, u32[]{:S(2)}) collective-permute-start(f32[3,66,1]{2,1,0:T(8,128)S(1)} %get-tuple-element.132), channel_id=1, source_target_pairs={{1,0},{2,1},{3,2},{4,3},{5,4},{6,5},{7,6},{8,7},{9,8},{10,9},{11,1... | collective-permute-start | bytes 2384 | tf_op jit(solution)/shard_map/ppermute | solution.py:25
  117.7 17.2 %collective-permute-start.6 = (f32[66,1]{1,0:T(8,128)}, f32[66,1]{1,0:T(8,128)S(1)}, u32[]{:S(2)}, u32[]{:S(2)}) collective-permute-start(f32[66,1]{1,0:T(8,128)} %get-tuple-element.146), channel_id=1, source_target_pairs={{1,0},{2,1},{3,2},{4,3},{5,4},{6,5},{7,6},{8,7},{9,8},{10,9},{11,1... | collective-permute-start | bytes 800 | tf_op jit(solution)/shard_map/ppermute | solution.py:25
  119.0 16.0 %collective-permute-start.7 = (f32[66,1]{1,0:T(8,128)}, f32[66,1]{1,0:T(8,128)S(1)}, u32[]{:S(2)}, u32[]{:S(2)}) collective-permute-start(f32[66,1]{1,0:T(8,128)} %get-tuple-element.147), channel_id=1, source_target_pairs={{0,1},{1,2},{2,3},{3,4},{4,5},{5,6},{6,7},{7,8},{8,9},{9,10},{10,1... | collective-permute-start | bytes 800 | tf_op jit(solution)/shard_map/ppermute | solution.py:24
  128.8 6.2 %copy-start.1 = (f32[64,1024]{1,0:T(8,128)S(1)}, f32[64,1024]{1,0:T(8,128)}, u32[]{:S(2)}) copy-start(f32[64,1024]{1,0:T(8,128)} %param.19) | copy-start | bytes 786436
  128.8 6.2 %copy-start.8 = (f32[66,1026]{1,0:T(8,128)S(1)}, f32[66,1026]{1,0:T(8,128)}, u32[]{:S(2)}) copy-start(f32[66,1026]{1,0:T(8,128)} %get-tuple-element.116) | copy-start | bytes 812596
  128.8 6.2 %copy-start.9 = (f32[66,1026]{1,0:T(8,128)S(1)}, f32[66,1026]{1,0:T(8,128)}, u32[]{:S(2)}) copy-start(f32[66,1026]{1,0:T(8,128)} %get-tuple-element.53) | copy-start | bytes 812596
  128.8 6.2 %copy-start.11 = (pred[64,1024]{1,0:T(8,128)(4,1)S(1)}, pred[64,1024]{1,0:T(8,128)(4,1)}, u32[]{:S(2)}) copy-start(pred[64,1024]{1,0:T(8,128)(4,1)} %get-tuple-element.158) | copy-start | bytes 196612
  128.8 6.2 %copy-start.12 = (pred[64,1024]{1,0:T(8,128)(4,1)S(1)}, pred[64,1024]{1,0:T(8,128)(4,1)}, u32[]{:S(2)}) copy-start(pred[64,1024]{1,0:T(8,128)(4,1)} %get-tuple-element.159) | copy-start | bytes 196612
  159.3 6.1 %collective-permute-start.8 = (f32[3,1,1024]{2,1,0:T(1,128)S(1)}, f32[3,1,1024]{2,1,0:T(1,128)S(1)}, u32[]{:S(2)}, u32[]{:S(2)}) collective-permute-start(f32[3,1,1024]{2,1,0:T(1,128)S(1)} %get-tuple-element.144), channel_id=1, source_target_pairs={{0,16},{16,32},{32,48},{48,64},{64,80},{80,96},{96,112},{1,17},{17... | collective-permute-start | bytes 36872 | tf_op jit(solution)/shard_map/ppermute | solution.py:24
  163.5 5.0 collective-permute-start.9
  168.6 0.9 copy-start.6
  169.7 75.8 %collective-permute-start.10 = (f32[3,66,1]{2,1,0:T(8,128)S(1)}, f32[3,66,1]{2,1,0:T(8,128)S(1)}, u32[]{:S(2)}, u32[]{:S(2)}) collective-permute-start(f32[3,66,1]{2,1,0:T(8,128)S(1)} %get-tuple-element.131), channel_id=1, source_target_pairs={{0,1},{1,2},{2,3},{3,4},{4,5},{5,6},{6,7},{7,8},{8,9},{9,10},{10,1... | collective-permute-start | bytes 2384 | tf_op jit(solution)/shard_map/ppermute | solution.py:24
  173.3 72.1 %collective-permute-start.11 = (f32[3,66,1]{2,1,0:T(8,128)S(1)}, f32[3,66,1]{2,1,0:T(8,128)S(1)}, u32[]{:S(2)}, u32[]{:S(2)}) collective-permute-start(f32[3,66,1]{2,1,0:T(8,128)S(1)} %get-tuple-element.130), channel_id=1, source_target_pairs={{1,0},{2,1},{3,2},{4,3},{5,4},{6,5},{7,6},{8,7},{9,8},{10,9},{11,1... | collective-permute-start | bytes 2384 | tf_op jit(solution)/shard_map/ppermute | solution.py:25
  251.3 5.7 collective-permute-start.12
  255.1 5.0 collective-permute-start.13
  260.3 0.9 copy-start.3
  261.3 70.4 %collective-permute-start.14 = (f32[3,66,1]{2,1,0:T(8,128)S(1)}, f32[3,66,1]{2,1,0:T(8,128)S(1)}, u32[]{:S(2)}, u32[]{:S(2)}) collective-permute-start(f32[3,66,1]{2,1,0:T(8,128)S(1)} %get-tuple-element.129), channel_id=1, source_target_pairs={{0,1},{1,2},{2,3},{3,4},{4,5},{5,6},{6,7},{7,8},{8,9},{9,10},{10,1... | collective-permute-start | bytes 2384 | tf_op jit(solution)/shard_map/ppermute | solution.py:24
  262.9 68.8 %collective-permute-start.15 = (f32[3,66,1]{2,1,0:T(8,128)S(1)}, f32[3,66,1]{2,1,0:T(8,128)S(1)}, u32[]{:S(2)}, u32[]{:S(2)}) collective-permute-start(f32[3,66,1]{2,1,0:T(8,128)S(1)} %get-tuple-element.128), channel_id=1, source_target_pairs={{1,0},{2,1},{3,2},{4,3},{5,4},{6,5},{7,6},{8,7},{9,8},{10,9},{11,1... | collective-permute-start | bytes 2384 | tf_op jit(solution)/shard_map/ppermute | solution.py:25
  337.6 5.4 collective-permute-start.16
  341.0 5.0 collective-permute-start.17
  346.1 0.9 copy-start.4
  347.1 70.6 %collective-permute-start.18 = (f32[3,66,1]{2,1,0:T(8,128)S(1)}, f32[3,66,1]{2,1,0:T(8,128)S(1)}, u32[]{:S(2)}, u32[]{:S(2)}) collective-permute-start(f32[3,66,1]{2,1,0:T(8,128)S(1)} %get-tuple-element.127), channel_id=1, source_target_pairs={{0,1},{1,2},{2,3},{3,4},{4,5},{5,6},{6,7},{7,8},{8,9},{9,10},{10,1... | collective-permute-start | bytes 2384 | tf_op jit(solution)/shard_map/ppermute | solution.py:24
  348.7 69.1 %collective-permute-start.19 = (f32[3,66,1]{2,1,0:T(8,128)S(1)}, f32[3,66,1]{2,1,0:T(8,128)S(1)}, u32[]{:S(2)}, u32[]{:S(2)}) collective-permute-start(f32[3,66,1]{2,1,0:T(8,128)S(1)} %get-tuple-element.126), channel_id=1, source_target_pairs={{1,0},{2,1},{3,2},{4,3},{5,4},{6,5},{7,6},{8,7},{9,8},{10,9},{11,1... | collective-permute-start | bytes 2384 | tf_op jit(solution)/shard_map/ppermute | solution.py:25
  423.7 5.3 collective-permute-start.20
  427.1 5.0 collective-permute-start.21
  432.2 0.9 copy-start.5
  433.2 70.6 %collective-permute-start.22 = (f32[3,66,1]{2,1,0:T(8,128)S(1)}, f32[3,66,1]{2,1,0:T(8,128)S(1)}, u32[]{:S(2)}, u32[]{:S(2)}) collective-permute-start(f32[3,66,1]{2,1,0:T(8,128)S(1)} %get-tuple-element.125), channel_id=1, source_target_pairs={{0,1},{1,2},{2,3},{3,4},{4,5},{5,6},{6,7},{7,8},{8,9},{9,10},{10,1... | collective-permute-start | bytes 2384 | tf_op jit(solution)/shard_map/ppermute | solution.py:24
  435.3 68.5 %collective-permute-start.23 = (f32[3,66,1]{2,1,0:T(8,128)S(1)}, f32[3,66,1]{2,1,0:T(8,128)S(1)}, u32[]{:S(2)}, u32[]{:S(2)}) collective-permute-start(f32[3,66,1]{2,1,0:T(8,128)S(1)} %get-tuple-element.124), channel_id=1, source_target_pairs={{1,0},{2,1},{3,2},{4,3},{5,4},{6,5},{7,6},{8,7},{9,8},{10,9},{11,1... | collective-permute-start | bytes 2384 | tf_op jit(solution)/shard_map/ppermute | solution.py:25
  509.7 5.1 collective-permute-start.24
  512.9 5.0 collective-permute-start.25
  518.0 0.9 copy-start.2
  519.1 70.9 %collective-permute-start.26 = (f32[3,66,1]{2,1,0:T(8,128)S(1)}, f32[3,66,1]{2,1,0:T(8,128)S(1)}, u32[]{:S(2)}, u32[]{:S(2)}) collective-permute-start(f32[3,66,1]{2,1,0:T(8,128)S(1)} %get-tuple-element.123), channel_id=1, source_target_pairs={{0,1},{1,2},{2,3},{3,4},{4,5},{5,6},{6,7},{7,8},{8,9},{9,10},{10,1... | collective-permute-start | bytes 2384 | tf_op jit(solution)/shard_map/ppermute | solution.py:24
  521.2 68.8 %collective-permute-start.27 = (f32[3,66,1]{2,1,0:T(8,128)S(1)}, f32[3,66,1]{2,1,0:T(8,128)S(1)}, u32[]{:S(2)}, u32[]{:S(2)}) collective-permute-start(f32[3,66,1]{2,1,0:T(8,128)S(1)} %get-tuple-element.122), channel_id=1, source_target_pairs={{1,0},{2,1},{3,2},{4,3},{5,4},{6,5},{7,6},{8,7},{9,8},{10,9},{11,1... | collective-permute-start | bytes 2384 | tf_op jit(solution)/shard_map/ppermute | solution.py:25
where the time goes:
time: 605 us; the launch traced here: 597 us
  blocking collectives  405 us (67%)
  starting transfers between devices  83.8 us (14%)
  other arithmetic  61.1 us (10%)
  local copies, waits for them, and re-layouts  25.1 us (4%)
  waiting for transfers between devices  15.4 us (3%)
  between operations  6.48 us (1%)
    pmax x6, blocking collectives, top_speed(): return lax.pmax(jnp.max(wave_speed(state)), ('row', 'col'))  405 us
    ppermute x14, starting transfers between devices, with_halo(): before = lax.ppermute(last, axis, up)  45.4 us
    reduce_max x6, other arithmetic, top_speed(): return lax.pmax(jnp.max(wave_speed(state)), ('row', 'col'))  31.4 us
    ppermute x14, starting transfers between devices, with_halo(): after = lax.ppermute(initial, axis, down)  22.5 us
    ppermute x14, waiting for transfers between devices, with_halo(): after = lax.ppermute(initial, axis, down)  15.4 us
  transfers between devices with their start and end apart: 30, of which 5 were waited for; matrix products, arithmetic and copies ran while one was open for 4% of the time, Pallas kernels for 0%

commit v1 on v0

v1 whole, which is shorter than its diff:
```python
import jax
import jax.numpy as jnp
from jax import lax
from jax.experimental import pallas as pl
from jax.experimental.pallas import tpu as pltpu
from jax.sharding import PartitionSpec as P

ITERS = 6
GRAVITY = 9.81
CELL_SIZE = 10.0
COURANT = 0.4
DEPTH_FLOOR = 0.05
BURN_LOSS = 1.5
BURN_SMOOTH = 0.5

LOGICAL = pl.DeviceIdType.LOGICAL
F32 = jnp.float32
BF16 = jnp.bfloat16

HOPS = (0, 1, 2, 1)
OFFSETS = sorted(
    [
        (x, core, z, y)
        for x in range(4)
        for core in range(2)
        for z in range(4)
        for y in range(4)
        if (x, core, z, y) != (0, 0, 0, 0)
    ],
    key=lambda o: (-(HOPS[o[0]] + HOPS[o[2]] + HOPS[o[3]]), -o[1]),
)
PEERS = len(OFFSETS)
DEVICES = PEERS + 1

CG = 8
TR = 64
PADR = TR + 16
TOP = 8


def approx_recip(value):
    guess = pl.reciprocal(value, approx=True)
    return guess * (2.0 - value * guess)


def root(value):
    safe = jnp.maximum(value, 1e-30)
    return safe * lax.rsqrt(safe)


def lanes(shape):
    return lax.broadcasted_iota(jnp.int32, shape, len(shape) - 1)


def nt_dot(a, b):
    return lax.dot_general(a, b, (((1,), (1,)), ((), ())), preferred_element_type=F32)


def kernel(
    refl_hbm, kid_hbm, dest_hbm, block_hbm, weight_hbm, depth_hbm, terrain_hbm, rain_hbm, burn_hbm, land_hbm,
    infil_tab, rough_tab,
    depth_out, east_out, north_out,
    refl, kid, dest, block, weight, rain, burn, land,
    state, bed, derived, drag_k, rate, infil, rough2, slope_e, slope_n,
    burn_index, outgoing, incoming, label_tile, label_out, label_in, label_q,
    max_out, max_in, row_out, row_in, col_out, col_in,
    in_sem, bulk_sem, halo_send, halo_recv, max_send, max_recv, out_sem,
):
    my_row, my_col = lax.axis_index("row"), lax.axis_index("col")
    rows_n, cols_n = 8, 16
    me = my_row * cols_n + my_col
    x, core, z, y = my_row // 2, lax.rem(my_row, 2), my_col // 4, lax.rem(my_col, 4)
    xs = [lax.rem(x + d, 4) * 32 for d in range(4)]
    cores = [lax.rem(core + d, 2) * 16 for d in range(2)]
    zs = [lax.rem(z + d, 4) * 4 for d in range(4)]
    ys = [lax.rem(y + d, 4) for d in range(4)]
    xc = [[a + b for b in cores] for a in xs]
    zy = [[a + b for b in ys] for a in zs]

    def target(o):
        return xc[o[0]][o[1]] + zy[o[2]][o[3]]

    south_dev = lax.rem(my_row + 1, rows_n) * cols_n + my_col
    north_dev = lax.rem(my_row + rows_n - 1, rows_n) * cols_n + my_col
    east_dev = my_row * cols_n + lax.rem(my_col + 1, cols_n)
    west_dev = my_row * cols_n + lax.rem(my_col + cols_n - 1, cols_n)

    def grid_copies(src, dst_of, sem):
        return [
            pltpu.make_async_copy(src.at[:, pl.ds(c * 128, 128)], dst_of(c), sem) for c in range(CG)
        ]

    loads = {
        "dest": [pltpu.make_async_copy(dest_hbm, dest, in_sem.at[0])],
        "kid": [pltpu.make_async_copy(kid_hbm, kid, in_sem.at[1])],
        "block": [pltpu.make_async_copy(block_hbm, block, in_sem.at[2])],
        "refl": [pltpu.make_async_copy(refl_hbm, refl, in_sem.at[3])],
        "weight": [pltpu.make_async_copy(weight_hbm, weight, in_sem.at[4])],
    }
    tile_rows = pl.ds(TOP, TR)
    grids = {
        "depth": (depth_hbm, lambda c: state.at[0, c + 1, tile_rows], 5),
        "terrain": (terrain_hbm, lambda c: bed.at[c + 1, tile_rows], 6),
        "land": (land_hbm, lambda c: land.at[c], 7),
        "burn": (burn_hbm, lambda c: burn.at[c], 8),
        "rain": (rain_hbm, lambda c: rain.at[c], 9),
    }
    for name, (src, dst_of, slot) in grids.items():
        loads[name] = [
            pltpu.make_async_copy(src.at[:, pl.ds(c * 128, 128)], dst_of(c), in_sem.at[slot + 5 * c])
            for c in range(CG)
        ]
    for name in ("dest", "block", "kid", "refl", "weight", "depth", "terrain", "land", "burn", "rain"):
        for copy in loads[name]:
            copy.start()

    def arrive(name):
        for copy in loads[name]:
            copy.wait()

    barrier = pltpu.get_barrier_semaphore()
    for o in OFFSETS:
        pl.semaphore_signal(barrier, inc=1, device_id=target(o), device_id_type=LOGICAL)

    edge = jnp.zeros((8, 128), F32)
    wide = jnp.zeros((PADR, 128), F32)

    def clear(c, _):
        state[1, c] = wide
        state[2, c] = wide
        for ref in (state.at[0], bed):
            ref[c, pl.ds(0, 8), :] = edge
            ref[c, pl.ds(TOP + TR, 8), :] = edge
        return 0

    lax.fori_loop(0, CG + 2, clear, 0)
    for c in (0, CG + 1):
        state[0, c] = wide
        bed[c] = wide

    arrive("dest")
    arrive("block")
    arrive("kid")
    dest_row = dest[...]
    blocks = dest_row.shape[1]
    member = lax.broadcasted_iota(jnp.int32, (DEVICES, blocks), 0) == dest_row
    member_f = jnp.where(member, 1.0, 0.0).astype(F32)
    member_b = member_f.astype(BF16)
    upper = jnp.where(
        lax.broadcasted_iota(jnp.int32, (blocks, blocks), 0) <= lanes((blocks, blocks)), 1.0, 0.0
    ).astype(BF16)
    counts = jnp.dot(member_b, upper, preferred_element_type=F32)
    rank = jnp.sum(member_f * counts, axis=0, keepdims=True) - 1.0
    position = dest_row.astype(F32) * 8.0 + rank

    block_row = block[...]
    high = (block_row // 16).astype(F32)
    low = lax.rem(block_row, 16).astype(F32)
    line = lax.broadcasted_iota(jnp.int32, (128, blocks), 0)
    by_rank = jnp.where(line.astype(F32) == rank, high, jnp.where(line.astype(F32) - 8.0 == rank, low, 0.0))
    label_tile[...] = nt_dot(member_b, by_rank.astype(BF16))

    arrive("refl")

    def index_chunk(i, _):
        rows = pl.ds(pl.multiple_of(i * 64, 64), 64)
        bands = [refl[b, rows, :].astype(F32) for b in range(4)]
        pre = (bands[0] - bands[1]) / (bands[0] + bands[1])
        post = (bands[2] - bands[3]) / (bands[2] + bands[3])
        burn_index[rows, :] = (pre - post).astype(BF16)
        return 0

    lax.fori_loop(0, blocks // 64, index_chunk, 0)

    arrive("weight")
    kid_lines = jnp.broadcast_to(kid[...].astype(F32), (128, blocks)).astype(BF16)
    stacked = weight[...].reshape(8 * 128, 128)

    def send_chunk(i, _):
        want = (lax.broadcasted_iota(jnp.int32, (128, blocks), 0) + i * 128).astype(F32)
        pick = jnp.where(want == position, 1.0, 0.0).astype(BF16)
        rows = jnp.dot(pick, burn_index[...], preferred_element_type=F32)
        which = nt_dot(pick, kid_lines)
        spread = jnp.concatenate(
            [jnp.where(which == float(k), rows, 0.0).astype(BF16) for k in range(8)], axis=1
        )
        result = jnp.dot(spread, stacked, preferred_element_type=F32)
        outgoing[pl.ds(pl.multiple_of(i * 16, 16), 16)] = result.reshape(16, 8, 128)
        return 0

    lax.fori_loop(0, DEVICES * 8 // 128, send_chunk, 0)

    arrive("depth")

    def deepest(c, best):
        return jnp.maximum(best, jnp.max(state[0, c + 1, tile_rows, :].reshape(8, 8, 128), axis=0))

    best = lax.fori_loop(0, CG, deepest, jnp.zeros((8, 128), F32))
    best = jnp.max(jnp.max(best, axis=0, keepdims=True), axis=1, keepdims=True)
    lane_row = lanes((1, 128))

    def label_line(i, _):
        label_out[i] = jnp.where(lane_row < 16, label_tile[pl.ds(i, 1), :], best)
        return 0

    lax.fori_loop(0, DEVICES, label_line, 0)

    lane_tile = lanes((8, 128))

    def pack(fields, it):
        for f, ref in enumerate(fields):
            for c in range(CG):
                row_out[it, 0, f * CG + c, :] = ref[c + 1, TOP, :]
                row_out[it, 1, f * CG + c, :] = ref[c + 1, TOP + TR - 1, :]
        first = jnp.zeros((8, 128), F32)
        last = jnp.zeros((8, 128), F32)
        for f, ref in enumerate(fields):
            for r in range(8):
                spot = r * 4 + f
                rows = pl.ds(TOP + r * 8, 8)
                first = jnp.where(lane_tile == spot, pltpu.roll(ref[1, rows, :], spot, 1), first)
                last = jnp.where(lane_tile == spot, pltpu.roll(ref[CG, rows, :], spot + 1, 1), last)
        col_out[it, 0] = first
        col_out[it, 1] = last

    def halo_copies(it):
        moves = (
            (row_out, row_in, 0, 1, north_dev, 0),
            (row_out, row_in, 1, 0, south_dev, 1),
            (col_out, col_in, 0, 1, west_dev, 2),
            (col_out, col_in, 1, 0, east_dev, 3),
        )
        return [
            pltpu.make_async_remote_copy(
                src_ref=src.at[it, a],
                dst_ref=dst.at[it, b],
                send_sem=halo_send.at[it, s],
                recv_sem=halo_recv.at[it, s],
                device_id=dev,
                device_id_type=LOGICAL,
            )
            for src, dst, a, b, dev, s in moves
        ]

    keep = (
        jnp.where(my_row > 0, 1.0, 0.0).astype(F32),
        jnp.where(my_row < rows_n - 1, 1.0, 0.0).astype(F32),
        jnp.where(my_col > 0, 1.0, 0.0).astype(F32),
        jnp.where(my_col < cols_n - 1, 1.0, 0.0).astype(F32),
    )

    def unpack(fields, it):
        for f, ref in enumerate(fields):
            for c in range(CG):
                ref[c + 1, TOP - 1, :] = row_in[it, 0, f * CG + c, :] * keep[0]
                ref[c + 1, TOP + TR, :] = row_in[it, 1, f * CG + c, :] * keep[1]
        west = col_in[it, 0] * keep[2]
        east = col_in[it, 1] * keep[3]
        for f, ref in enumerate(fields):
            for r in range(8):
                spot = r * 4 + f
                rows = pl.ds(TOP + r * 8, 8)
                ref[0, rows, :] = pltpu.roll(west, 127 - spot, 1)
                ref[CG + 1, rows, :] = pltpu.roll(east, (128 - spot) % 128, 1)

    state_refs = [state.at[f] for f in range(3)]
    arrive("terrain")
    pack([state.at[0], bed], 0)

    pl.semaphore_wait(barrier, PEERS)

    def data_copy(k, o):
        there = target(o)
        return pltpu.make_async_remote_copy(
            src_ref=outgoing.at[there],
            dst_ref=incoming.at[k],
            send_sem=bulk_sem.at[0],
            recv_sem=bulk_sem.at[1],
            device_id=there,
            device_id_type=LOGICAL,
        )

    def label_copy(k, o):
        there = target(o)
        return pltpu.make_async_remote_copy(
            src_ref=label_out.at[there],
            dst_ref=label_in.at[k],
            send_sem=bulk_sem.at[2],
            recv_sem=bulk_sem.at[3],
            device_id=there,
            device_id_type=LOGICAL,
        )

    for copy in halo_copies(0):
        copy.start()
    for k, o in enumerate(OFFSETS):
        data_copy(k, o).start()
        for j in (2 * k, 2 * k + 1):
            if j < PEERS:
                label_copy(j, OFFSETS[j]).start()
    incoming[PEERS] = outgoing[me]
    label_in[PEERS] = label_out[me]

    arrive("land")
    arrive("burn")
    arrive("rain")

    def classes(c, _):
        for r in range(8):
            rows = pl.ds(r * 8, 8)
            kind = land[c, rows, :]
            burned = burn[c, rows, :].astype(F32)
            soak = jnp.full((8, 128), infil_tab[0], F32)
            manning = jnp.full((8, 128), rough_tab[0], F32)
            for entry in range(1, 16):
                hit = kind == entry
                soak = jnp.where(hit, infil_tab[entry], soak)
                manning = jnp.where(hit, rough_tab[entry], manning)
            manning = manning * (1.0 - BURN_SMOOTH * burned)
            infil[c, rows, :] = soak
            rough2[c, rows, :] = GRAVITY * manning * manning
        return 0

    lax.fori_loop(0, CG, classes, 0)

    def west_of(ref, c, rows):
        return pltpu.roll(jnp.where(lane_tile == 127, ref[c, rows, :], ref[c + 1, rows, :]), 1, 1)

    def east_of(ref, c, rows):
        return pltpu.roll(jnp.where(lane_tile == 0, ref[c + 2, rows, :], ref[c + 1, rows, :]), 127, 1)

    def derive(c, rows, r):
        depth, east, north = state[0, c, rows, :], state[1, c, rows, :], state[2, c, rows, :]
        floored = jnp.maximum(depth, DEPTH_FLOOR)
        inverse = approx_recip(floored)
        east_speed, north_speed = east * inverse, north * inverse
        celerity = root(GRAVITY * depth)
        pressure = (0.5 * GRAVITY) * depth * depth
        derived[0, c, rows, :] = east * east_speed + pressure
        derived[1, c, rows, :] = east * north_speed
        derived[2, c, rows, :] = north * north_speed + pressure
        derived[3, c, rows, :] = jnp.abs(east_speed) + celerity
        derived[4, c, rows, :] = jnp.abs(north_speed) + celerity
        if r is not None:
            inner = pl.ds(r * 8, 8)
            magnitude = root(east_speed * east_speed + north_speed * north_speed)
            power = jnp.exp((-4.0 / 3.0) * jnp.log(floored))
            drag_k[c - 1, inner, :] = rough2[c - 1, inner, :] * magnitude * power

    def derive_inside():
        def group(c, _):
            for r in range(8):
                derive(c + 1, pl.ds(TOP + r * 8, 8), r)
            return 0

        lax.fori_loop(0, CG, group, 0)

    def derive_edges():
        def group(c, _):
            derive(c + 1, pl.ds(0, 8), None)
            derive(c + 1, pl.ds(TOP + TR, 8), None)
            return 0

        lax.fori_loop(0, CG, group, 0)
        for c in (0, CG + 1):
            for r in range(8):
                derive(c, pl.ds(TOP + r * 8, 8), None)

    def flux():
        def group(c, _):
            for r in range(8):
                inner = pl.ds(r * 8, 8)
                rows, above, below = (pl.ds(TOP + r * 8 + s, 8) for s in (0, -1, 1))
                q = [state[f, c + 1, rows, :] for f in range(3)]
                flux_e = [q[1], derived[0, c + 1, rows, :], derived[1, c + 1, rows, :]]
                total = []
                refs = [state.at[0], state.at[1], state.at[2], derived.at[0], derived.at[1], derived.at[3]]
                d_w, e_w, n_w, a_w, b_w, reach_w = [west_of(ref, c, rows) for ref in refs]
                d_e, e_e, n_e, a_e, b_e, reach_e = [east_of(ref, c, rows) for ref in refs]
                reach = derived[3, c + 1, rows, :]
                face_w, face_e = jnp.maximum(reach, reach_w), jnp.maximum(reach, reach_e)
                for mid, q_w, q_e, f_w, f_e in (
                    (q[0], d_w, d_e, e_w, e_e),
                    (q[1], e_w, e_e, a_w, a_e),
                    (q[2], n_w, n_e, b_w, b_e),
                ):
                    total.append((f_e - f_w) - face_e * (q_e - mid) + face_w * (mid - q_w))
                q_n = [state[f, c + 1, above, :] for f in range(3)]
                q_s = [state[f, c + 1, below, :] for f in range(3)]
                reach = derived[4, c + 1, rows, :]
                face_n = jnp.maximum(reach, derived[4, c + 1, above, :])
                face_s = jnp.maximum(reach, derived[4, c + 1, below, :])
                g_n = [q_n[2], derived[1, c + 1, above, :], derived[2, c + 1, above, :]]
                g_s = [q_s[2], derived[1, c + 1, below, :], derived[2, c + 1, below, :]]
                for f in range(3):
                    total[f] = total[f] + (
                        (g_s[f] - g_n[f]) - face_s * (q_s[f] - q[f]) + face_n * (q[f] - q_n[f])
                    )
                scale = 0.5 / CELL_SIZE
                rate[0, c, inner, :] = rain[c, inner, :] - scale * total[0]
                rate[1, c, inner, :] = -scale * total[1] - q[0] * slope_e[c, inner, :]
                rate[2, c, inner, :] = -scale * total[2] - q[0] * slope_n[c, inner, :]
            return 0

        lax.fori_loop(0, CG, group, 0)

    def apply(top):
        time_step = (COURANT * CELL_SIZE) / top

        def group(c, best):
            for r in range(8):
                inner, rows = pl.ds(r * 8, 8), pl.ds(TOP + r * 8, 8)
                wet = state[0, c + 1, rows, :] + time_step * rate[0, c, inner, :]
                depth = jnp.maximum(wet - time_step * infil[c, inner, :], 0.0)
                slow = approx_recip(1.0 + time_step * drag_k[c, inner, :])
                east = (state[1, c + 1, rows, :] + time_step * rate[1, c, inner, :]) * slow
                north = (state[2, c + 1, rows, :] + time_step * rate[2, c, inner, :]) * slow
                state[0, c + 1, rows, :] = depth
                state[1, c + 1, rows, :] = east
                state[2, c + 1, rows, :] = north
                inverse = approx_recip(jnp.maximum(depth, DEPTH_FLOOR))
                speed = jnp.maximum(jnp.abs(east), jnp.abs(north)) * inverse + root(GRAVITY * depth)
                best = jnp.maximum(best, speed)
            return best

        best = lax.fori_loop(0, CG, group, jnp.zeros((8, 128), F32))
        return jnp.max(best, axis=0, keepdims=True)

    derive_inside()
    for copy in halo_copies(0):
        copy.wait()
    unpack([state.at[0], bed], 0)

    def slopes(c, _):
        for r in range(8):
            inner, rows = pl.ds(r * 8, 8), pl.ds(TOP + r * 8, 8)
            scale = GRAVITY / (2.0 * CELL_SIZE)
            slope_e[c, inner, :] = scale * (east_of(bed, c, rows) - west_of(bed, c, rows))
            slope_n[c, inner, :] = scale * (
                bed[c + 1, pl.ds(TOP + r * 8 + 1, 8), :] - bed[c + 1, pl.ds(TOP + r * 8 - 1, 8), :]
            )
        return 0

    lax.fori_loop(0, CG, slopes, 0)
    derive_edges()
    flux()

    def bulk_wait(buf, s):
        ref = buf.at[pl.ds(0, PEERS)]
        pltpu.make_async_remote_copy(
            src_ref=ref,
            dst_ref=ref,
            send_sem=bulk_sem.at[s],
            recv_sem=bulk_sem.at[s + 1],
            device_id=east_dev,
            device_id_type=LOGICAL,
        ).wait()

    bulk_wait(label_in, 2)

    def label_back(i, _):
        label_tile[pl.ds(i, 1), :] = label_in[i]
        return 0

    lax.fori_loop(0, DEVICES, label_back, 0)
    labels = label_tile[...]
    deep = jnp.max(jnp.max(jnp.where(lanes((DEVICES, 128)) < 16, 0.0, labels), axis=0, keepdims=True), axis=1, keepdims=True)
    top = root(GRAVITY * deep)
    turned = labels.T
    number = turned[0:8] * 16.0 + turned[8:16]
    spots = lax.broadcasted_iota(jnp.int32, (512, 128), 0)
    spots = (lax.rem(spots, TR) * CG + spots // TR).astype(F32)
    for q in range(8):
        label_q[:, pl.ds(q * 128, 128)] = jnp.where(spots == number[q : q + 1, :], 1.0, 0.0).astype(BF16)

    bulk_wait(incoming, 0)
    parts = []
    for q in range(8):
        rows = incoming[:, q, :]
        coarse = rows.astype(BF16)
        parts.append(jnp.concatenate([coarse, (rows - coarse.astype(F32)).astype(BF16)], axis=1))
    both = jnp.dot(label_q[...], jnp.concatenate(parts, axis=0), preferred_element_type=F32)
    severity = (both[:, :128] + both[:, 128:]).reshape(CG, TR, 128)
    infil[...] = infil[...] * jnp.exp(-BURN_LOSS * burn[...].astype(F32) * jnp.maximum(severity, 0.0))
    local = apply(top)

    def step(it, local):
        max_out[it] = local
        for k, o in enumerate(OFFSETS):
            if k == 40:
                pack(state_refs, it)
                for copy in halo_copies(it):
                    copy.start()
            pltpu.make_async_remote_copy(
                src_ref=max_out.at[it],
                dst_ref=max_in.at[it, k],
                send_sem=max_send.at[it],
                recv_sem=max_recv.at[it],
                device_id=target(o),
                device_id_type=LOGICAL,
            ).start()
        derive_inside()
        for copy in halo_copies(it):
            copy.wait()
        unpack(state_refs, it)
        derive_edges()
        flux()
        pltpu.make_async_remote_copy(
            src_ref=max_in.at[it],
            dst_ref=max_in.at[it],
            send_sem=max_send.at[it],
            recv_sem=max_recv.at[it],
            device_id=east_dev,
            device_id_type=LOGICAL,
        ).wait()
        top = jnp.maximum(local, jnp.max(max_in[it], axis=0))
        return apply(jnp.max(top, axis=1, keepdims=True))

    lax.fori_loop(1, ITERS, step, local)

    stores = [
        pltpu.make_async_copy(state.at[f, c + 1, tile_rows], out.at[:, pl.ds(c * 128, 128)], out_sem.at[f, c])
        for f, out in enumerate((depth_out, east_out, north_out))
        for c in range(CG)
    ]
    for copy in stores:
        copy.start()
    for copy in stores:
        copy.wait()


def body(
    reflectance, kernel_id, dest_device, dest_block, regrid_weight, depth0, terrain, rain, burn_mask, land_class,
    infil_table, rough_table,
):
    blocks = reflectance.shape[1]
    grid = jax.ShapeDtypeStruct(depth0.shape, F32)
    cells = (CG, TR, 128)
    padded = (CG + 2, PADR, 128)
    anywhere = pl.BlockSpec(memory_space=pl.ANY)
    scalars = pl.BlockSpec(memory_space=pltpu.SMEM)
    return pl.pallas_call(
        kernel,
        out_shape=(grid, grid, grid),
        in_specs=[anywhere] * 10 + [scalars] * 2,
        out_specs=(anywhere,) * 3,
        scratch_shapes=[
            pltpu.VMEM(reflectance.shape, BF16),
            pltpu.VMEM((1, blocks), jnp.int32),
            pltpu.VMEM((1, blocks), jnp.int32),
            pltpu.VMEM((1, blocks), jnp.int32),
            pltpu.VMEM(regrid_weight.shape, BF16),
            pltpu.VMEM(cells, F32),
            pltpu.VMEM(cells, jnp.int32),
            pltpu.VMEM(cells, jnp.int32),
            pltpu.VMEM((3,) + padded, F32),
            pltpu.VMEM(padded, F32),
            pltpu.VMEM((5,) + padded, F32),
            pltpu.VMEM(cells, F32),
            pltpu.VMEM((3,) + cells, F32),
            pltpu.VMEM(cells, F32),
            pltpu.VMEM(cells, F32),
            pltpu.VMEM(cells, F32),
            pltpu.VMEM(cells, F32),
            pltpu.VMEM((blocks, 128), BF16),
            pltpu.VMEM((DEVICES, 8, 128), F32),
            pltpu.VMEM((DEVICES, 8, 128), F32),
            pltpu.VMEM((DEVICES, 128), F32),
            pltpu.VMEM((DEVICES, 1, 128), F32),
            pltpu.VMEM((DEVICES, 1, 128), F32),
            pltpu.VMEM((512, 1024), BF16),
            pltpu.VMEM((ITERS, 1, 128), F32),
            pltpu.VMEM((ITERS, PEERS, 1, 128), F32),
            pltpu.VMEM((ITERS, 2, 24, 128), F32),
            pltpu.VMEM((ITERS, 2, 24, 128), F32),
            pltpu.VMEM((ITERS, 2, 8, 128), F32),
            pltpu.VMEM((ITERS, 2, 8, 128), F32),
            pltpu.SemaphoreType.DMA((5 + 5 * CG,)),
            pltpu.SemaphoreType.DMA((4,)),
            pltpu.SemaphoreType.DMA((ITERS, 4)),
            pltpu.SemaphoreType.DMA((ITERS, 4)),
            pltpu.SemaphoreType.DMA((ITERS,)),
            pltpu.SemaphoreType.DMA((ITERS,)),
            pltpu.SemaphoreType.DMA((3, CG)),
        ],
        compiler_params=pltpu.CompilerParams(
            collective_id=0, has_side_effects=True, vmem_limit_bytes=48 * 2**20
        ),
        cost_estimate=pl.CostEstimate(flops=10**9, bytes_accessed=3 * 10**6, transcendentals=10**6),
    )(
        reflectance,
        kernel_id.reshape(1, blocks),
        dest_device.reshape(1, blocks),
        dest_block.reshape(1, blocks),
        regrid_weight,
        depth0,
        terrain,
        rain,
        burn_mask,
        land_class,
        infil_table,
        rough_table,
    )


def solution(mesh):
    both = ("row", "col")
    grid = P("row", "col")
    return jax.shard_map(
        body,
        mesh=mesh,
        in_specs=(P(None, both, None), P(both), P(both, None), P(both), P()) + (grid,) * 5 + (P(), P()),
        out_specs=(grid, grid, grid),
        check_vma=False,
    )
```

time: 605 us -> 70.9 us (0.12); the launches traced: 597 us -> 70.5 us
  blocking collectives: 405 us -> 0 us
  starting transfers between devices: 83.8 us -> 0 us
  other arithmetic: 61.1 us -> 0 us
  Pallas kernels: 0 us -> 59.6 us
  waiting for transfers between devices: 15.4 us -> 0 us
  local copies, waits for them, and re-layouts: 25.1 us -> 10.2 us
    pmax x6 -> x0, blocking collectives: 405 us -> none  [top_speed(): return lax.pmax(jnp.max(wave_speed(state)), ('row', 'col'))]
    ppermute x28 -> x0, starting transfers between devices: 67.8 us -> none  [the longest x14 45.4 us: with_halo(): before = lax.ppermute(last, axis, up)]
    pallas_call x0 -> x1, Pallas kernels: none -> 59.6 us  [body(): pl.pallas_call(kernel, out_shape=(grid, grid, grid), in_specs=[anywhere]...]
    reduce_max x6 -> x0, other arithmetic: 31.4 us -> none  [top_speed(): return lax.pmax(jnp.max(wave_speed(state)), ('row', 'col'))]
    all_to_all x2 -> x0, starting transfers between devices: 16 us -> none  [the longest x1 10.6 us: body(): lax.all_to_all(labels.reshape(device_count, capacity), ('row', 'col'), sp...]
    ppermute x28 -> x0, waiting for transfers between devices: 15.4 us -> none  [the longest x14 15.4 us: with_halo(): after = lax.ppermute(initial, axis, down)]
    concatenate x6 -> x0, local copies, waits for them, and re-layouts: 8.92 us -> none  [with_halo(): value = jnp.concatenate([before, value, after], axis=dim)]
    div x13 -> x0, other arithmetic: 7.31 us -> none  [the longest x6 4.45 us: advance(): (face_east[:, 1:-1, 1:] - face_east[:, 1:-1, :-1] + face_north[:, 1:, 1:-...]
  transfers between devices with their start and end apart: 30 -> 0, of which waited for: 5 -> 0; matrix products, arithmetic and copies ran while one was open for 4% -> 0% of each run, Pallas kernels for 0% -> 0%
where the time goes in v1:
time: 70.9 us; the launch traced here: 70.5 us
  Pallas kernels  59.6 us (84%)
  local copies, waits for them, and re-layouts  10.2 us (14%)
    pallas_call x1, Pallas kernels, body(): pl.pallas_call(kernel, out_shape=(grid, grid, grid), in_specs=[anywhere]...  59.6 us
    unnamed x27, local copies, waits for them, and re-layouts  10.2 us

profile of v1, /device:TPU:1, one launch (start us, length us, event | category | flops | bytes accessed | tf_op | source)
XLA Modules:
  0.0 70.5 jit_solution(12507974733557714165)
XLA Ops:
  0.6 0.0 copy-start.8
  0.6 0.0 copy-start.7
  0.7 0.0 copy-start.10
  0.7 0.0 copy-start.11
  0.7 0.6 copy-done.8
  1.3 0.0 copy-done.7
  1.3 0.0 copy-done.10
  1.3 0.0 copy-done.11
  1.3 0.0 copy-start
  1.3 1.0 %copy-done = bf16[4,512,128]{2,1,0:T(8,128)(2,1)S(1)} copy-done((bf16[4,512,128]{2,1,0:T(8,128)(2,1)S(1)}, bf16[4,512,128]{2,1,0:T(8,128)(2,1)}, u32[]{:S(2)}) %copy-start) | copy-done | bytes 524312
  2.4 0.0 copy-start.1
  2.4 0.9 %copy-done.1 = bf16[8,128,128]{2,1,0:T(8,128)(2,1)S(1)} copy-done((bf16[8,128,128]{2,1,0:T(8,128)(2,1)S(1)}, bf16[8,128,128]{2,1,0:T(8,128)(2,1)}, u32[]{:S(2)}) %copy-start.1) | copy-done | bytes 262168
  3.3 0.0 copy-start.2
  3.3 0.9 %copy-done.2 = f32[64,1024]{1,0:T(8,128)S(1)} copy-done((f32[64,1024]{1,0:T(8,128)S(1)}, f32[64,1024]{1,0:T(8,128)}, u32[]{:S(2)}) %copy-start.2) | copy-done | bytes 262168
  4.3 0.0 copy-start.3
  4.3 0.9 %copy-done.3 = f32[64,1024]{1,0:T(8,128)S(1)} copy-done((f32[64,1024]{1,0:T(8,128)S(1)}, f32[64,1024]{1,0:T(8,128)}, u32[]{:S(2)}) %copy-start.3) | copy-done | bytes 262168
  5.2 0.0 copy-start.4
  5.2 0.9 %copy-done.4 = f32[64,1024]{1,0:T(8,128)S(1)} copy-done((f32[64,1024]{1,0:T(8,128)S(1)}, f32[64,1024]{1,0:T(8,128)}, u32[]{:S(2)}) %copy-start.4) | copy-done | bytes 262168
  6.2 0.0 copy-start.5
  6.2 0.9 %copy-done.5 = s32[64,1024]{1,0:T(8,128)S(1)} copy-done((s32[64,1024]{1,0:T(8,128)S(1)}, s32[64,1024]{1,0:T(8,128)}, u32[]{:S(2)}) %copy-start.5) | copy-done | bytes 262168
  7.1 0.0 copy-start.6
  7.1 0.9 %copy-done.6 = s32[64,1024]{1,0:T(8,128)S(1)} copy-done((s32[64,1024]{1,0:T(8,128)S(1)}, s32[64,1024]{1,0:T(8,128)}, u32[]{:S(2)}) %copy-start.6) | copy-done | bytes 262168
  8.1 0.0 copy-start.9
  8.1 0.7 copy-done.9
  8.8 59.6 %shard_map.139 = (f32[64,1024]{1,0:T(8,128)S(1)}, f32[64,1024]{1,0:T(8,128)S(1)}, f32[64,1024]{1,0:T(8,128)S(1)}) custom-call(bf16[4,512,128]{2,1,0:T(8,128)(2,1)S(1)} %copy-done, s32[1,512]{1,0:T(1,128)S(1)} %bitcast.3, s32[1,512]{1,0:T(1,128)S(1)} %bitcast.4, s32[1,512]{1,0:T(1,128)S(1)} %bitcast.5, bf16[8,128,128]{2,1,0:T(8,128)(2,1)S(1)} %copy-done.1, ...), custom_call_target="tpu_custom_call" | custom-call | flops 1000000000 | bytes 3000000 | tf_op jit(solution)/shard_map/pallas_call | solution.py:542
  68.4 0.7 %copy.18 = f32[64,1024]{1,0:T(8,128)} copy(f32[64,1024]{1,0:T(8,128)S(1)} %get-tuple-element.6) | data formatting | bytes 524288
  69.1 0.7 copy.19
  69.8 0.7 copy.20
Async XLA Ops:
  0.6 0.7 copy-start.8
  0.6 0.7 copy-start.7
  0.7 0.7 copy-start.10
  0.7 0.7 copy-start.11
  1.3 1.0 %copy-start = (bf16[4,512,128]{2,1,0:T(8,128)(2,1)S(1)}, bf16[4,512,128]{2,1,0:T(8,128)(2,1)}, u32[]{:S(2)}) copy-start(bf16[4,512,128]{2,1,0:T(8,128)(2,1)} %refl_hbm.1) | copy-start | bytes 1572868
  2.4 0.9 %copy-start.1 = (bf16[8,128,128]{2,1,0:T(8,128)(2,1)S(1)}, bf16[8,128,128]{2,1,0:T(8,128)(2,1)}, u32[]{:S(2)}) copy-start(bf16[8,128,128]{2,1,0:T(8,128)(2,1)} %weight_hbm.1) | copy-start | bytes 786436
  3.3 0.9 %copy-start.2 = (f32[64,1024]{1,0:T(8,128)S(1)}, f32[64,1024]{1,0:T(8,128)}, u32[]{:S(2)}) copy-start(f32[64,1024]{1,0:T(8,128)} %depth_hbm.1) | copy-start | bytes 786436
  4.3 0.9 %copy-start.3 = (f32[64,1024]{1,0:T(8,128)S(1)}, f32[64,1024]{1,0:T(8,128)}, u32[]{:S(2)}) copy-start(f32[64,1024]{1,0:T(8,128)} %terrain_hbm.1) | copy-start | bytes 786436
  5.2 0.9 %copy-start.4 = (f32[64,1024]{1,0:T(8,128)S(1)}, f32[64,1024]{1,0:T(8,128)}, u32[]{:S(2)}) copy-start(f32[64,1024]{1,0:T(8,128)} %rain_hbm.1) | copy-start | bytes 786436
  6.2 0.9 %copy-start.5 = (s32[64,1024]{1,0:T(8,128)S(1)}, s32[64,1024]{1,0:T(8,128)}, u32[]{:S(2)}) copy-start(s32[64,1024]{1,0:T(8,128)} %burn_hbm.1) | copy-start | bytes 786436
  7.1 0.9 %copy-start.6 = (s32[64,1024]{1,0:T(8,128)S(1)}, s32[64,1024]{1,0:T(8,128)}, u32[]{:S(2)}) copy-start(s32[64,1024]{1,0:T(8,128)} %land_hbm.1) | copy-start | bytes 786436
  8.1 0.7 copy-start.9

commit v2 on v1

--- a/solution.py
+++ b/solution.py
@@ -36,11 +36,13 @@
 TR = 64
 PADR = TR + 16
 TOP = 8
-
-
-def approx_recip(value):
-    guess = pl.reciprocal(value, approx=True)
-    return guess * (2.0 - value * guess)
+GROUPS = 4
+GROUP = DEVICES // GROUPS
+LINES = 9
+
+
+def inverse_of(value):
+    return pltpu.reciprocal(value, approx=True)
 
 
 def root(value):
@@ -58,13 +60,13 @@
 
 def kernel(
     refl_hbm, kid_hbm, dest_hbm, block_hbm, weight_hbm, depth_hbm, terrain_hbm, rain_hbm, burn_hbm, land_hbm,
-    infil_tab, rough_tab,
-    depth_out, east_out, north_out,
-    refl, kid, dest, block, weight, rain, burn, land,
-    state, bed, derived, drag_k, rate, infil, rough2, slope_e, slope_n,
-    burn_index, outgoing, incoming, label_tile, label_out, label_in, label_q,
+    infil_hbm, rough_hbm,
+    state, rate, drag_k, infil, top_out,
+    infil_tab, rough_tab, refl, kid, dest, block, weight, rain, burn, land,
+    bed, derived, rough2, fade, slope_e, slope_n,
+    kid_lines, spread, outgoing, incoming, gathered,
     max_out, max_in, row_out, row_in, col_out, col_in,
-    in_sem, bulk_sem, halo_send, halo_recv, max_send, max_recv, out_sem,
+    in_sem, bulk_send, bulk_recv, halo_send, halo_recv, max_send, max_recv,
 ):
     my_row, my_col = lax.axis_index("row"), lax.axis_index("col")
     rows_n, cols_n = 8, 16
@@ -96,6 +98,10 @@
         "block": [pltpu.make_async_copy(block_hbm, block, in_sem.at[2])],
         "refl": [pltpu.make_async_copy(refl_hbm, refl, in_sem.at[3])],
         "weight": [pltpu.make_async_copy(weight_hbm, weight, in_sem.at[4])],
+        "tables": [
+            pltpu.make_async_copy(infil_hbm, infil_tab, in_sem.at[45]),
+            pltpu.make_async_copy(rough_hbm, rough_tab, in_sem.at[46]),
+        ],
     }
     tile_rows = pl.ds(TOP, TR)
     grids = {
@@ -110,9 +116,12 @@
             pltpu.make_async_copy(src.at[:, pl.ds(c * 128, 128)], dst_of(c), in_sem.at[slot + 5 * c])
             for c in range(CG)
         ]
-    for name in ("dest", "block", "kid", "refl", "weight", "depth", "terrain", "land", "burn", "rain"):
-        for copy in loads[name]:
-            copy.start()
+    def begin(*names):
+        for name in names:
+            for copy in loads[name]:
+                copy.start()
+
+    begin("dest", "refl", "block", "kid", "weight")
 
     def arrive(name):
         for copy in loads[name]:
@@ -121,6 +130,7 @@
     barrier = pltpu.get_barrier_semaphore()
     for o in OFFSETS:
         pl.semaphore_signal(barrier, inc=1, device_id=target(o), device_id_type=LOGICAL)
+    begin("depth", "terrain", "land", "burn", "rain", "tables")
 
     edge = jnp.zeros((8, 128), F32)
     wide = jnp.zeros((PADR, 128), F32)
@@ -151,44 +161,38 @@
     ).astype(BF16)
     counts = jnp.dot(member_b, upper, preferred_element_type=F32)
     rank = jnp.sum(member_f * counts, axis=0, keepdims=True) - 1.0
-    position = dest_row.astype(F32) * 8.0 + rank
 
     block_row = block[...]
     high = (block_row // 16).astype(F32)
     low = lax.rem(block_row, 16).astype(F32)
     line = lax.broadcasted_iota(jnp.int32, (128, blocks), 0)
     by_rank = jnp.where(line.astype(F32) == rank, high, jnp.where(line.astype(F32) - 8.0 == rank, low, 0.0))
-    label_tile[...] = nt_dot(member_b, by_rank.astype(BF16))
-
+    numbers = nt_dot(member_b, by_rank.astype(BF16))
+
+    kid_lines[...] = jnp.broadcast_to(kid[...].astype(F32), (128, blocks)).T
     arrive("refl")
 
     def index_chunk(i, _):
         rows = pl.ds(pl.multiple_of(i * 64, 64), 64)
         bands = [refl[b, rows, :].astype(F32) for b in range(4)]
-        pre = (bands[0] - bands[1]) / (bands[0] + bands[1])
-        post = (bands[2] - bands[3]) / (bands[2] + bands[3])
-        burn_index[rows, :] = (pre - post).astype(BF16)
+        pre = (bands[0] - bands[1]) * inverse_of(bands[0] + bands[1])
+        post = (bands[2] - bands[3]) * inverse_of(bands[2] + bands[3])
+        index = (pre - post).astype(BF16).astype(F32)
+        which = kid_lines[rows, :]
+        for k in range(8):
+            spread[rows, pl.ds(k * 128, 128)] = jnp.where(which == float(k), index, 0.0).astype(BF16)
         return 0
 
-    lax.fori_loop(0, blocks // 64, index_chunk, 0)
-
+    lax.fori_loop(0, blocks // 64, index_chunk, 0, unroll=2)
     arrive("weight")
-    kid_lines = jnp.broadcast_to(kid[...].astype(F32), (128, blocks)).astype(BF16)
-    stacked = weight[...].reshape(8 * 128, 128)
-
-    def send_chunk(i, _):
-        want = (lax.broadcasted_iota(jnp.int32, (128, blocks), 0) + i * 128).astype(F32)
-        pick = jnp.where(want == position, 1.0, 0.0).astype(BF16)
-        rows = jnp.dot(pick, burn_index[...], preferred_element_type=F32)
-        which = nt_dot(pick, kid_lines)
-        spread = jnp.concatenate(
-            [jnp.where(which == float(k), rows, 0.0).astype(BF16) for k in range(8)], axis=1
-        )
-        result = jnp.dot(spread, stacked, preferred_element_type=F32)
-        outgoing[pl.ds(pl.multiple_of(i * 16, 16), 16)] = result.reshape(16, 8, 128)
-        return 0
-
-    lax.fori_loop(0, DEVICES * 8 // 128, send_chunk, 0)
+    regridded = jnp.dot(spread[...], weight[...].reshape(8 * 128, 128), preferred_element_type=F32)
+    coarse = regridded.astype(BF16)
+    halves = jnp.concatenate([coarse, (regridded - coarse.astype(F32)).astype(BF16)], axis=1)
+
+    for q in range(8):
+        pick = jnp.where(rank == float(q), member_f, 0.0).astype(BF16)
+        both = jnp.dot(pick, halves, preferred_element_type=F32)
+        outgoing[:, q, :] = both[:, :128] + both[:, 128:]
 
     arrive("depth")
 
@@ -197,13 +201,7 @@
 
     best = lax.fori_loop(0, CG, deepest, jnp.zeros((8, 128), F32))
     best = jnp.max(jnp.max(best, axis=0, keepdims=True), axis=1, keepdims=True)
-    lane_row = lanes((1, 128))
-
-    def label_line(i, _):
-        label_out[i] = jnp.where(lane_row < 16, label_tile[pl.ds(i, 1), :], best)
-        return 0
-
-    lax.fori_loop(0, DEVICES, label_line, 0)
+    outgoing[:, 8, :] = jnp.where(lanes((DEVICES, 128)) < 16, numbers, best)
 
     lane_tile = lanes((8, 128))
 
@@ -269,41 +267,24 @@
 
     pl.semaphore_wait(barrier, PEERS)
 
-    def data_copy(k, o):
-        there = target(o)
-        return pltpu.make_async_remote_copy(
-            src_ref=outgoing.at[there],
-            dst_ref=incoming.at[k],
-            send_sem=bulk_sem.at[0],
-            recv_sem=bulk_sem.at[1],
-            device_id=there,
-            device_id_type=LOGICAL,
-        )
-
-    def label_copy(k, o):
-        there = target(o)
-        return pltpu.make_async_remote_copy(
-            src_ref=label_out.at[there],
-            dst_ref=label_in.at[k],
-            send_sem=bulk_sem.at[2],
-            recv_sem=bulk_sem.at[3],
-            device_id=there,
-            device_id_type=LOGICAL,
-        )
-
     for copy in halo_copies(0):
         copy.start()
     for k, o in enumerate(OFFSETS):
-        data_copy(k, o).start()
-        for j in (2 * k, 2 * k + 1):
-            if j < PEERS:
-                label_copy(j, OFFSETS[j]).start()
+        there = target(o)
+        pltpu.make_async_remote_copy(
+            src_ref=outgoing.at[there],
+            dst_ref=incoming.at[k],
+            send_sem=bulk_send.at[k // GROUP],
+            recv_sem=bulk_recv.at[k // GROUP],
+            device_id=there,
+            device_id_type=LOGICAL,
+        ).start()
     incoming[PEERS] = outgoing[me]
-    label_in[PEERS] = label_out[me]
 
     arrive("land")
     arrive("burn")
     arrive("rain")
+    arrive("tables")
 
     def classes(c, _):
         for r in range(8):
@@ -318,6 +299,7 @@
                 manning = jnp.where(hit, rough_tab[entry], manning)
             manning = manning * (1.0 - BURN_SMOOTH * burned)
             infil[c, rows, :] = soak
+            fade[c, rows, :] = -BURN_LOSS * burned
             rough2[c, rows, :] = GRAVITY * manning * manning
         return 0
 
@@ -332,7 +314,7 @@
     def derive(c, rows, r):
         depth, east, north = state[0, c, rows, :], state[1, c, rows, :], state[2, c, rows, :]
         floored = jnp.maximum(depth, DEPTH_FLOOR)
-        inverse = approx_recip(floored)
+        inverse = inverse_of(floored)
         east_speed, north_speed = east * inverse, north * inverse
         celerity = root(GRAVITY * depth)
         pressure = (0.5 * GRAVITY) * depth * depth
@@ -366,9 +348,10 @@
             for r in range(8):
                 derive(c, pl.ds(TOP + r * 8, 8), None)
 
-    def flux():
-        def group(c, _):
-            for r in range(8):
+    def flux(columns, first, row_groups):
+        def group(i, _):
+            c = first(i)
+            for r in row_groups:
                 inner = pl.ds(r * 8, 8)
                 rows, above, below = (pl.ds(TOP + r * 8 + s, 8) for s in (0, -1, 1))
                 q = [state[f, c + 1, rows, :] for f in range(3)]
@@ -402,92 +385,114 @@
                 rate[2, c, inner, :] = -scale * total[2] - q[0] * slope_n[c, inner, :]
             return 0
 
-        lax.fori_loop(0, CG, group, 0)
+        lax.fori_loop(0, columns, group, 0)
+
+    def flux_inside():
+        flux(CG - 2, lambda i: i + 1, range(1, 7))
+
+    def flux_edges():
+        flux(CG - 2, lambda i: i + 1, (0, 7))
+        flux(2, lambda i: i * (CG - 1), range(8))
 
     def apply(top):
         time_step = (COURANT * CELL_SIZE) / top
 
         def group(c, best):
             for r in range(8):
-                inner, rows = pl.ds(r * 8, 8), pl.ds(TOP + r * 8, 8)
-                wet = state[0, c + 1, rows, :] + time_step * rate[0, c, inner, :]
-                depth = jnp.maximum(wet - time_step * infil[c, inner, :], 0.0)
-                slow = approx_recip(1.0 + time_step * drag_k[c, inner, :])
-                east = (state[1, c + 1, rows, :] + time_step * rate[1, c, inner, :]) * slow
-                north = (state[2, c + 1, rows, :] + time_step * rate[2, c, inner, :]) * slow
+                rows = pl.ds(TOP + r * 8, 8)
+                depth, east, north = advance(time_step, state, rate, drag_k, infil, c, r)
                 state[0, c + 1, rows, :] = depth
                 state[1, c + 1, rows, :] = east
                 state[2, c + 1, rows, :] = north
-                inverse = approx_recip(jnp.maximum(depth, DEPTH_FLOOR))
+                inverse = inverse_of(jnp.maximum(depth, DEPTH_FLOOR))
                 speed = jnp.maximum(jnp.abs(east), jnp.abs(north)) * inverse + root(GRAVITY * depth)
                 best = jnp.maximum(best, speed)
             return best
 
-        best = lax.fori_loop(0, CG, group, jnp.zeros((8, 128), F32))
+        best = lax.fori_loop(0, CG, group, jnp.zeros((8, 128), F32), unroll=4)
         return jnp.max(best, axis=0, keepdims=True)
 
-    derive_inside()
     for copy in halo_copies(0):
         copy.wait()
     unpack([state.at[0], bed], 0)
 
-    def slopes(c, _):
+    def from_rest(c, _):
         for r in range(8):
-            inner, rows = pl.ds(r * 8, 8), pl.ds(TOP + r * 8, 8)
-            scale = GRAVITY / (2.0 * CELL_SIZE)
-            slope_e[c, inner, :] = scale * (east_of(bed, c, rows) - west_of(bed, c, rows))
-            slope_n[c, inner, :] = scale * (
-                bed[c + 1, pl.ds(TOP + r * 8 + 1, 8), :] - bed[c + 1, pl.ds(TOP + r * 8 - 1, 8), :]
-            )
+            inner = pl.ds(r * 8, 8)
+            rows, above, below = (pl.ds(TOP + r * 8 + s, 8) for s in (0, -1, 1))
+            gain = GRAVITY / (2.0 * CELL_SIZE)
+            tilt_e = gain * (east_of(bed, c, rows) - west_of(bed, c, rows))
+            tilt_n = gain * (bed[c + 1, below, :] - bed[c + 1, above, :])
+            slope_e[c, inner, :] = tilt_e
+            slope_n[c, inner, :] = tilt_n
+            mid = state[0, c + 1, rows, :]
+            reach = root(GRAVITY * mid)
+            scale = 0.5 / CELL_SIZE
+            total = 0.0
+            rates = []
+            for low, high, tilt in (
+                (west_of(state.at[0], c, rows), east_of(state.at[0], c, rows), tilt_e),
+                (state[0, c + 1, above, :], state[0, c + 1, below, :], tilt_n),
+            ):
+                face_low = jnp.maximum(reach, root(GRAVITY * low))
+                face_high = jnp.maximum(reach, root(GRAVITY * high))
+                total = total - face_high * (high - mid) + face_low * (mid - low)
+                rates.append((-0.5 * scale * GRAVITY) * (high * high - low * low) - mid * tilt)
+            rate[0, c, inner, :] = rain[c, inner, :] - scale * total
+            rate[1, c, inner, :] = rates[0]
+            rate[2, c, inner, :] = rates[1]
+            drag_k[c, inner, :] = jnp.zeros((8, 128), F32)
         return 0
 
-    lax.fori_loop(0, CG, slopes, 0)
-    derive_edges()
-    flux()
-
-    def bulk_wait(buf, s):
-        ref = buf.at[pl.ds(0, PEERS)]
+    lax.fori_loop(0, CG, from_rest, 0)
+
+    spots = lax.broadcasted_iota(jnp.int32, (512, 128), 0)
+    spots = (lax.rem(spots, TR) * CG + spots // TR).astype(F32)
+    sub16, lane16 = lax.broadcasted_iota(jnp.int32, (16, 128), 0), lanes((16, 128))
+    join = jnp.where(lane16 == sub16, 16.0, jnp.where(lane16 == sub16 + 8, 1.0, 0.0)).astype(BF16)
+    share = 128 // GROUP
+    deep = jnp.zeros((GROUP, 128), F32)
+    for g in range(GROUPS):
+        there = incoming.at[pl.ds(g * GROUP, min(GROUP, PEERS - g * GROUP))]
         pltpu.make_async_remote_copy(
-            src_ref=ref,
-            dst_ref=ref,
-            send_sem=bulk_sem.at[s],
-            recv_sem=bulk_sem.at[s + 1],
+            src_ref=there,
+            dst_ref=there,
+            send_sem=bulk_send.at[g],
+            recv_sem=bulk_recv.at[g],
             device_id=east_dev,
             device_id_type=LOGICAL,
         ).wait()
-
-    bulk_wait(label_in, 2)
-
-    def label_back(i, _):
-        label_tile[pl.ds(i, 1), :] = label_in[i]
-        return 0
-
-    lax.fori_loop(0, DEVICES, label_back, 0)
-    labels = label_tile[...]
-    deep = jnp.max(jnp.max(jnp.where(lanes((DEVICES, 128)) < 16, 0.0, labels), axis=0, keepdims=True), axis=1, keepdims=True)
+        sources = pl.ds(g * GROUP, GROUP)
+        lines = incoming[sources, 8, :]
+        deep = jnp.maximum(deep, jnp.where(lanes((GROUP, 128)) < 16, 0.0, lines))
+        number = nt_dot(join, jnp.concatenate([lines.astype(BF16)] * share, axis=0))[:8]
+        sub8, lane8 = lax.broadcasted_iota(jnp.int32, (8, 128), 0), lanes((8, 128))
+        picks, parts = [], []
+        for h in range(8 // share):
+            wanted = sub8 == h * share + lane8 // GROUP
+            row = jnp.sum(jnp.where(wanted, number, 0.0), axis=0, keepdims=True)
+            picks.append(jnp.where(spots == row, 1.0, 0.0).astype(BF16))
+        for q in range(8):
+            rows = incoming[sources, q, :]
+            coarse = rows.astype(BF16)
+            parts.append(jnp.concatenate([coarse, (rows - coarse.astype(F32)).astype(BF16)], axis=1))
+        part = jnp.dot(jnp.concatenate(picks, axis=1), jnp.concatenate(parts, axis=0), preferred_element_type=F32)
+        if g == 0:
+            gathered[...] = part
+        elif g < GROUPS - 1:
+            gathered[...] += part
+        else:
+            part = part + gathered[...]
+    severity = (part[:, :128] + part[:, 128:]).reshape(CG, TR, 128)
+    infil[...] = infil[...] * jnp.exp(fade[...] * jnp.maximum(severity, 0.0))
+    deep = jnp.max(jnp.max(deep, axis=0, keepdims=True), axis=1, keepdims=True)
     top = root(GRAVITY * deep)
-    turned = labels.T
-    number = turned[0:8] * 16.0 + turned[8:16]
-    spots = lax.broadcasted_iota(jnp.int32, (512, 128), 0)
-    spots = (lax.rem(spots, TR) * CG + spots // TR).astype(F32)
-    for q in range(8):
-        label_q[:, pl.ds(q * 128, 128)] = jnp.where(spots == number[q : q + 1, :], 1.0, 0.0).astype(BF16)
-
-    bulk_wait(incoming, 0)
-    parts = []
-    for q in range(8):
-        rows = incoming[:, q, :]
-        coarse = rows.astype(BF16)
-        parts.append(jnp.concatenate([coarse, (rows - coarse.astype(F32)).astype(BF16)], axis=1))
-    both = jnp.dot(label_q[...], jnp.concatenate(parts, axis=0), preferred_element_type=F32)
-    severity = (both[:, :128] + both[:, 128:]).reshape(CG, TR, 128)
-    infil[...] = infil[...] * jnp.exp(-BURN_LOSS * burn[...].astype(F32) * jnp.maximum(severity, 0.0))
     local = apply(top)
 
-    def step(it, local):
+    def before_apply(it, local):
         max_out[it] = local
         for k, o in enumerate(OFFSETS):
-            if k == 40:
+            if k == 14:
                 pack(state_refs, it)
                 for copy in halo_copies(it):
                     copy.start()
@@ -500,11 +505,12 @@
                 device_id_type=LOGICAL,
             ).start()
         derive_inside()
+        flux_inside()
         for copy in halo_copies(it):
             copy.wait()
         unpack(state_refs, it)
         derive_edges()
-        flux()
+        flux_edges()
         pltpu.make_async_remote_copy(
             src_ref=max_in.at[it],
             dst_ref=max_in.at[it],
@@ -514,17 +520,36 @@
             device_id_type=LOGICAL,
         ).wait()
         top = jnp.maximum(local, jnp.max(max_in[it], axis=0))
-        return apply(jnp.max(top, axis=1, keepdims=True))
-
-    lax.fori_loop(1, ITERS, step, local)
-
-    stores = [
-        pltpu.make_async_copy(state.at[f, c + 1, tile_rows], out.at[:, pl.ds(c * 128, 128)], out_sem.at[f, c])
-        for f, out in enumerate((depth_out, east_out, north_out))
-        for c in range(CG)
-    ]
-    for copy in stores:
-        copy.start()
+        return jnp.max(top, axis=1, keepdims=True)
+
+    def step(it, local):
+        return apply(before_apply(it, local))
+
+    local = lax.fori_loop(1, ITERS - 1, step, local)
+    top_out[...] = jnp.broadcast_to(before_apply(ITERS - 1, local), (8, 128))
+
+
+def advance(time_step, state, rate, drag_k, infil, c, r):
+    inner, rows = pl.ds(r * 8, 8), pl.ds(TOP + r * 8, 8)
+    wet = state[0, c + 1, rows, :] + time_step * rate[0, c, inner, :]
+    depth = jnp.maximum(wet - time_step * infil[c, inner, :], 0.0)
+    slow = inverse_of(1.0 + time_step * drag_k[c, inner, :])
+    east = (state[1, c + 1, rows, :] + time_step * rate[1, c, inner, :]) * slow
+    north = (state[2, c + 1, rows, :] + time_step * rate[2, c, inner, :]) * slow
+    return depth, east, north
+
+
+def last_step(state, rate, drag_k, infil, top, depth_out, east_out, north_out, panels, out_sem):
+    time_step = (COURANT * CELL_SIZE) / top[...]
+    stores = []
+    for c in range(CG):
+        for r in range(8):
+            for f, value in enumerate(advance(time_step, state, rate, drag_k, infil, c, r)):
+                panels[f, c, pl.ds(r * 8, 8), :] = value
+        for f, out in enumerate((depth_out, east_out, north_out)):
+            copy = pltpu.make_async_copy(panels.at[f, c], out.at[:, pl.ds(c * 128, 128)], out_sem.at[f, c])
+            copy.start()
+            stores.append(copy)
     for copy in stores:
         copy.wait()
 
@@ -538,56 +563,8 @@
     cells = (CG, TR, 128)
     padded = (CG + 2, PADR, 128)
     anywhere = pl.BlockSpec(memory_space=pl.ANY)
-    scalars = pl.BlockSpec(memory_space=pltpu.SMEM)
-    return pl.pallas_call(
-        kernel,
-        out_shape=(grid, grid, grid),
-        in_specs=[anywhere] * 10 + [scalars] * 2,
-        out_specs=(anywhere,) * 3,
-        scratch_shapes=[
-            pltpu.VMEM(reflectance.shape, BF16),
-            pltpu.VMEM((1, blocks), jnp.int32),
-            pltpu.VMEM((1, blocks), jnp.int32),
-            pltpu.VMEM((1, blocks), jnp.int32),
-            pltpu.VMEM(regrid_weight.shape, BF16),
-            pltpu.VMEM(cells, F32),
-            pltpu.VMEM(cells, jnp.int32),
-            pltpu.VMEM(cells, jnp.int32),
-            pltpu.VMEM((3,) + padded, F32),
-            pltpu.VMEM(padded, F32),
-            pltpu.VMEM((5,) + padded, F32),
-            pltpu.VMEM(cells, F32),
-            pltpu.VMEM((3,) + cells, F32),
-            pltpu.VMEM(cells, F32),
-            pltpu.VMEM(cells, F32),
-            pltpu.VMEM(cells, F32),
-            pltpu.VMEM(cells, F32),
-            pltpu.VMEM((blocks, 128), BF16),
-            pltpu.VMEM((DEVICES, 8, 128), F32),
-            pltpu.VMEM((DEVICES, 8, 128), F32),
-            pltpu.VMEM((DEVICES, 128), F32),
-            pltpu.VMEM((DEVICES, 1, 128), F32),
-            pltpu.VMEM((DEVICES, 1, 128), F32),
-            pltpu.VMEM((512, 1024), BF16),
-            pltpu.VMEM((ITERS, 1, 128), F32),
-            pltpu.VMEM((ITERS, PEERS, 1, 128), F32),
-            pltpu.VMEM((ITERS, 2, 24, 128), F32),
-            pltpu.VMEM((ITERS, 2, 24, 128), F32),
-            pltpu.VMEM((ITERS, 2, 8, 128), F32),
-            pltpu.VMEM((ITERS, 2, 8, 128), F32),
-            pltpu.SemaphoreType.DMA((5 + 5 * CG,)),
-            pltpu.SemaphoreType.DMA((4,)),
-            pltpu.SemaphoreType.DMA((ITERS, 4)),
-            pltpu.SemaphoreType.DMA((ITERS, 4)),
-            pltpu.SemaphoreType.DMA((ITERS,)),
-            pltpu.SemaphoreType.DMA((ITERS,)),
-            pltpu.SemaphoreType.DMA((3, CG)),
-        ],
-        compiler_params=pltpu.CompilerParams(
-            collective_id=0, has_side_effects=True, vmem_limit_bytes=48 * 2**20
-        ),
-        cost_estimate=pl.CostEstimate(flops=10**9, bytes_accessed=3 * 10**6, transcendentals=10**6),
-    )(
+    vmem = pl.BlockSpec(memory_space=pltpu.VMEM)
+    operands = (
         reflectance,
         kernel_id.reshape(1, blocks),
         dest_device.reshape(1, blocks),
@@ -601,6 +578,66 @@
         infil_table,
         rough_table,
     )
+    results = pl.pallas_call(
+        kernel,
+        out_shape=(
+            pltpu.VMEM((3,) + padded, F32),
+            pltpu.VMEM((3,) + cells, F32),
+            pltpu.VMEM(cells, F32),
+            pltpu.VMEM(cells, F32),
+            pltpu.VMEM((8, 128), F32),
+        ),
+        in_specs=[anywhere] * 12,
+        out_specs=(vmem,) * 5,
+        scratch_shapes=[
+            pltpu.SMEM(infil_table.shape, F32),
+            pltpu.SMEM(rough_table.shape, F32),
+            pltpu.VMEM(reflectance.shape, BF16),
+            pltpu.VMEM((1, blocks), jnp.int32),
+            pltpu.VMEM((1, blocks), jnp.int32),
+            pltpu.VMEM((1, blocks), jnp.int32),
+            pltpu.VMEM(regrid_weight.shape, BF16),
+            pltpu.VMEM(cells, F32),
+            pltpu.VMEM(cells, jnp.int32),
+            pltpu.VMEM(cells, jnp.int32),
+            pltpu.VMEM(padded, F32),
+            pltpu.VMEM((5,) + padded, F32),
+            pltpu.VMEM(cells, F32),
+            pltpu.VMEM(cells, F32),
+            pltpu.VMEM(cells, F32),
+            pltpu.VMEM(cells, F32),
+            pltpu.VMEM((blocks, 128), F32),
+            pltpu.VMEM((blocks, 8 * 128), BF16),
+            pltpu.VMEM((DEVICES, LINES, 128), F32),
+            pltpu.VMEM((DEVICES, LINES, 128), F32),
+            pltpu.VMEM((512, 256), F32),
+            pltpu.VMEM((ITERS, 1, 128), F32),
+            pltpu.VMEM((ITERS, PEERS, 1, 128), F32),
+            pltpu.VMEM((ITERS, 2, 24, 128), F32),
+            pltpu.VMEM((ITERS, 2, 24, 128), F32),
+            pltpu.VMEM((ITERS, 2, 8, 128), F32),
+            pltpu.VMEM((ITERS, 2, 8, 128), F32),
+            pltpu.SemaphoreType.DMA((7 + 5 * CG,)),
+            pltpu.SemaphoreType.DMA((GROUPS,)),
+            pltpu.SemaphoreType.DMA((GROUPS,)),
+            pltpu.SemaphoreType.DMA((ITERS, 4)),
+            pltpu.SemaphoreType.DMA((ITERS, 4)),
+            pltpu.SemaphoreType.DMA((ITERS,)),
+            pltpu.SemaphoreType.DMA((ITERS,)),
+        ],
+        compiler_params=pltpu.CompilerParams(
+            collective_id=0, has_side_effects=True, vmem_limit_bytes=48 * 2**20
+        ),
+        cost_estimate=pl.CostEstimate(flops=10**9, bytes_accessed=3 * 10**6, transcendentals=10**6),
+    )(*[pltpu.with_memory_space_constraint(operand, pltpu.HBM) for operand in operands])
+    return pl.pallas_call(
+        last_step,
+        out_shape=(grid, grid, grid),
+        in_specs=[vmem] * 5,
+        out_specs=(anywhere,) * 3,
+        scratch_shapes=[pltpu.VMEM((3,) + cells, F32), pltpu.SemaphoreType.DMA((3, CG))],
+        compiler_params=pltpu.CompilerParams(vmem_limit_bytes=4 * 2**20),
+    )(*[pltpu.with_memory_space_constraint(result, pltpu.VMEM) for result in results])
 
 
 def solution(mesh):

time: 70.9 us -> 55.8 us (0.79)
  local copies, waits for them, and re-layouts: 10.2 us -> 0 us
  Pallas kernels: 59.6 us -> 55.1 us
    unnamed x27 -> x0, local copies, waits for them, and re-layouts: 10.2 us -> none
    pallas_call x1 -> x2, Pallas kernels: 59.6 us -> 55.1 us  [the longest x1 54 us: body(): pl.pallas_call(kernel, out_shape=(pltpu.VMEM((3,) + padded, F32), pltpu.V...]
where the time goes in v2:
time: 55.8 us; the launch traced here: 55.7 us
  Pallas kernels  55.1 us (99%)
  between operations  0.64 us (1%)
    pallas_call x1, Pallas kernels, body(): pl.pallas_call(kernel, out_shape=(pltpu.VMEM((3,) + padded, F32), pltpu.V...  54 us

profile of v2, /device:TPU:1, one launch (start us, length us, event | category | flops | bytes accessed | tf_op | source)
XLA Modules:
  0.0 55.7 jit_solution(16806074035029008595)
XLA Ops:
  0.6 54.0 %shard_map.139 = (f32[3,10,80,128]{3,2,1,0:T(8,128)S(1)}, f32[3,8,64,128]{3,2,1,0:T(8,128)S(1)}, f32[8,64,128]{2,1,0:T(8,128)S(1)}, f32[8,64,128]{2,1,0:T(8,128)S(1)}, f32[8,128]{1,0:T(8,128)S(1)}) custom-call(bf16[4,512,128]{2,1,0:T(8,128)(2,1)} %refl_hbm.1, s32[1,512]{1,0:T(1,128)} %bitcast.3, s32[1,512]{1,0:T(1,128)} %bitcast.4, s32[1,512]{1,0:T(1,128)} %bitcast.5, ...), custom_call_target="tpu_custom_call" | custom-call | flops 1000000000 | bytes 3000000 | tf_op jit(solution)/shard_map/pallas_call | solution.py:581
  54.6 1.1 %shard_map.140 = (f32[64,1024]{1,0:T(8,128)}, f32[64,1024]{1,0:T(8,128)}, f32[64,1024]{1,0:T(8,128)}) custom-call(f32[3,10,80,128]{3,2,1,0:T(8,128)S(1)} %get-tuple-element.8.state, f32[3,8,64,128]{3,2,1,0:T(8,128)S(1)} %get-tuple-element.9.rate, f32[8,64,128]{2,1,0:T(8,128)S(1)} %get-tuple-element.10.drag_k, f32[8,64,128]{2,1,0:T(8,128)S(1)} %get-tuple-element.11.infil, ...), custom_call_target="tpu_custom_call" | custom-call | tf_op jit(solution)/shard_map/pallas_call | solution.py:633

commit v3 on v2

--- a/solution.py
+++ b/solution.py
@@ -30,14 +30,16 @@
     key=lambda o: (-(HOPS[o[0]] + HOPS[o[2]] + HOPS[o[3]]), -o[1]),
 )
 PEERS = len(OFFSETS)
+FAR = 14
 DEVICES = PEERS + 1
 
 CG = 8
 TR = 64
 PADR = TR + 16
 TOP = 8
-GROUPS = 4
-GROUP = DEVICES // GROUPS
+GROUPS = (64, 64)
+STARTS = [sum(GROUPS[:g]) for g in range(len(GROUPS))]
+GROUP_OF = [g for g, size in enumerate(GROUPS) for _ in range(size)]
 LINES = 9
 
 
@@ -61,8 +63,8 @@
 def kernel(
     refl_hbm, kid_hbm, dest_hbm, block_hbm, weight_hbm, depth_hbm, terrain_hbm, rain_hbm, burn_hbm, land_hbm,
     infil_hbm, rough_hbm,
-    state, rate, drag_k, infil, top_out,
-    infil_tab, rough_tab, refl, kid, dest, block, weight, rain, burn, land,
+    state, rate, drag_k, top_out,
+    infil, infil_tab, rough_tab, refl, kid, dest, block, weight, rain, burn, land,
     bed, derived, rough2, fade, slope_e, slope_n,
     kid_lines, spread, outgoing, incoming, gathered,
     max_out, max_in, row_out, row_in, col_out, col_in,
@@ -121,14 +123,15 @@
             for copy in loads[name]:
                 copy.start()
 
-    begin("dest", "refl", "block", "kid", "weight")
 
     def arrive(name):
         for copy in loads[name]:
             copy.wait()
 
     barrier = pltpu.get_barrier_semaphore()
-    for o in OFFSETS:
+    for k, o in enumerate(OFFSETS):
+        if k == FAR:
+            begin("dest", "refl", "block", "kid", "weight")
         pl.semaphore_signal(barrier, inc=1, device_id=target(o), device_id_type=LOGICAL)
     begin("depth", "terrain", "land", "burn", "rain", "tables")
 
@@ -274,8 +277,8 @@
         pltpu.make_async_remote_copy(
             src_ref=outgoing.at[there],
             dst_ref=incoming.at[k],
-            send_sem=bulk_send.at[k // GROUP],
-            recv_sem=bulk_recv.at[k // GROUP],
+            send_sem=bulk_send.at[GROUP_OF[k]],
+            recv_sem=bulk_recv.at[GROUP_OF[k]],
             device_id=there,
             device_id_type=LOGICAL,
         ).start()
@@ -380,7 +383,7 @@
                         (g_s[f] - g_n[f]) - face_s * (q_s[f] - q[f]) + face_n * (q[f] - q_n[f])
                     )
                 scale = 0.5 / CELL_SIZE
-                rate[0, c, inner, :] = rain[c, inner, :] - scale * total[0]
+                rate[0, c, inner, :] = rain[c, inner, :] - infil[c, inner, :] - scale * total[0]
                 rate[1, c, inner, :] = -scale * total[1] - q[0] * slope_e[c, inner, :]
                 rate[2, c, inner, :] = -scale * total[2] - q[0] * slope_n[c, inner, :]
             return 0
@@ -394,26 +397,34 @@
         flux(CG - 2, lambda i: i + 1, (0, 7))
         flux(2, lambda i: i * (CG - 1), range(8))
 
-    def apply(top):
-        time_step = (COURANT * CELL_SIZE) / top
-
-        def group(c, best):
+    def apply(top, it):
+        time_step = (COURANT * CELL_SIZE) * inverse_of(top)
+        best = first = last = jnp.zeros((8, 128), F32)
+        for c in range(CG):
             for r in range(8):
                 rows = pl.ds(TOP + r * 8, 8)
-                depth, east, north = advance(time_step, state, rate, drag_k, infil, c, r)
-                state[0, c + 1, rows, :] = depth
-                state[1, c + 1, rows, :] = east
-                state[2, c + 1, rows, :] = north
+                values = advance(time_step, state, rate, drag_k, c, r)
+                for f, value in enumerate(values):
+                    spot = r * 4 + f
+                    state[f, c + 1, rows, :] = value
+                    if r == 0:
+                        row_out[it, 0, f * CG + c, :] = value[0]
+                    if r == 7:
+                        row_out[it, 1, f * CG + c, :] = value[7]
+                    if c == 0:
+                        first = jnp.where(lane_tile == spot, pltpu.roll(value, spot, 1), first)
+                    if c == CG - 1:
+                        last = jnp.where(lane_tile == spot, pltpu.roll(value, spot + 1, 1), last)
+                depth, east, north = values
                 inverse = inverse_of(jnp.maximum(depth, DEPTH_FLOOR))
                 speed = jnp.maximum(jnp.abs(east), jnp.abs(north)) * inverse + root(GRAVITY * depth)
                 best = jnp.maximum(best, speed)
-            return best
-
-        best = lax.fori_loop(0, CG, group, jnp.zeros((8, 128), F32), unroll=4)
+        col_out[it, 0] = first
+        col_out[it, 1] = last
         return jnp.max(best, axis=0, keepdims=True)
 
     for copy in halo_copies(0):
-        copy.wait()
+        copy.wait_recv()
     unpack([state.at[0], bed], 0)
 
     def from_rest(c, _):
@@ -446,30 +457,33 @@
 
     lax.fori_loop(0, CG, from_rest, 0)
 
-    spots = lax.broadcasted_iota(jnp.int32, (512, 128), 0)
-    spots = (lax.rem(spots, TR) * CG + spots // TR).astype(F32)
-    sub16, lane16 = lax.broadcasted_iota(jnp.int32, (16, 128), 0), lanes((16, 128))
-    join = jnp.where(lane16 == sub16, 16.0, jnp.where(lane16 == sub16 + 8, 1.0, 0.0)).astype(BF16)
-    share = 128 // GROUP
-    deep = jnp.zeros((GROUP, 128), F32)
-    for g in range(GROUPS):
-        there = incoming.at[pl.ds(g * GROUP, min(GROUP, PEERS - g * GROUP))]
-        pltpu.make_async_remote_copy(
+    def group_copy(g):
+        there = incoming.at[pl.ds(STARTS[g], min(GROUPS[g], PEERS - STARTS[g]))]
+        return pltpu.make_async_remote_copy(
             src_ref=there,
             dst_ref=there,
             send_sem=bulk_send.at[g],
             recv_sem=bulk_recv.at[g],
             device_id=east_dev,
             device_id_type=LOGICAL,
-        ).wait()
-        sources = pl.ds(g * GROUP, GROUP)
+        )
+
+    spots = lax.broadcasted_iota(jnp.int32, (512, 128), 0)
+    spots = (lax.rem(spots, TR) * CG + spots // TR).astype(F32)
+    sub16, lane16 = lax.broadcasted_iota(jnp.int32, (16, 128), 0), lanes((16, 128))
+    join = jnp.where(lane16 == sub16, 16.0, jnp.where(lane16 == sub16 + 8, 1.0, 0.0)).astype(BF16)
+    deep = jnp.zeros((8, 128), F32)
+    for g, size in enumerate(GROUPS):
+        group_copy(g).wait_recv()
+        sources = pl.ds(STARTS[g], size)
+        share = 128 // size
         lines = incoming[sources, 8, :]
-        deep = jnp.maximum(deep, jnp.where(lanes((GROUP, 128)) < 16, 0.0, lines))
+        deep = jnp.maximum(deep, jnp.max(lines.reshape(size // 8, 8, 128), axis=0))
         number = nt_dot(join, jnp.concatenate([lines.astype(BF16)] * share, axis=0))[:8]
         sub8, lane8 = lax.broadcasted_iota(jnp.int32, (8, 128), 0), lanes((8, 128))
         picks, parts = [], []
         for h in range(8 // share):
-            wanted = sub8 == h * share + lane8 // GROUP
+            wanted = sub8 == h * share + lane8 // size
             row = jnp.sum(jnp.where(wanted, number, 0.0), axis=0, keepdims=True)
             picks.append(jnp.where(spots == row, 1.0, 0.0).astype(BF16))
         for q in range(8):
@@ -479,75 +493,87 @@
         part = jnp.dot(jnp.concatenate(picks, axis=1), jnp.concatenate(parts, axis=0), preferred_element_type=F32)
         if g == 0:
             gathered[...] = part
-        elif g < GROUPS - 1:
+        elif g < len(GROUPS) - 1:
             gathered[...] += part
         else:
             part = part + gathered[...]
     severity = (part[:, :128] + part[:, 128:]).reshape(CG, TR, 128)
-    infil[...] = infil[...] * jnp.exp(fade[...] * jnp.maximum(severity, 0.0))
+    soaked = infil[...] * jnp.exp(fade[...] * jnp.maximum(severity, 0.0))
+    infil[...] = soaked
+    rate[0] = rate[0] - soaked
+    deep = jnp.where(lanes((8, 128)) < 16, 0.0, deep)
     deep = jnp.max(jnp.max(deep, axis=0, keepdims=True), axis=1, keepdims=True)
     top = root(GRAVITY * deep)
-    local = apply(top)
+    def max_copy(it, part):
+        there = max_in.at[it, pl.ds(*((0, FAR), (FAR, PEERS - FAR))[part])]
+        return pltpu.make_async_remote_copy(
+            src_ref=there,
+            dst_ref=there,
+            send_sem=max_send.at[it, part],
+            recv_sem=max_recv.at[it, part],
+            device_id=east_dev,
+            device_id_type=LOGICAL,
+        )
 
     def before_apply(it, local):
         max_out[it] = local
         for k, o in enumerate(OFFSETS):
-            if k == 14:
-                pack(state_refs, it)
+            if k == FAR:
                 for copy in halo_copies(it):
                     copy.start()
             pltpu.make_async_remote_copy(
                 src_ref=max_out.at[it],
                 dst_ref=max_in.at[it, k],
-                send_sem=max_send.at[it],
-                recv_sem=max_recv.at[it],
+                send_sem=max_send.at[it, int(k >= FAR)],
+                recv_sem=max_recv.at[it, int(k >= FAR)],
                 device_id=target(o),
                 device_id_type=LOGICAL,
             ).start()
         derive_inside()
         flux_inside()
         for copy in halo_copies(it):
-            copy.wait()
+            copy.wait_recv()
         unpack(state_refs, it)
         derive_edges()
         flux_edges()
-        pltpu.make_async_remote_copy(
-            src_ref=max_in.at[it],
-            dst_ref=max_in.at[it],
-            send_sem=max_send.at[it],
-            recv_sem=max_recv.at[it],
-            device_id=east_dev,
-            device_id_type=LOGICAL,
-        ).wait()
-        top = jnp.maximum(local, jnp.max(max_in[it], axis=0))
+        max_copy(it, 1).wait_recv()
+        top = jnp.maximum(local, jnp.max(max_in[it, pl.ds(FAR, PEERS - FAR)], axis=0))
+        max_copy(it, 0).wait_recv()
+        top = jnp.maximum(top, jnp.max(max_in[it, pl.ds(0, FAR)], axis=0))
         return jnp.max(top, axis=1, keepdims=True)
 
-    def step(it, local):
-        return apply(before_apply(it, local))
-
-    local = lax.fori_loop(1, ITERS - 1, step, local)
-    top_out[...] = jnp.broadcast_to(before_apply(ITERS - 1, local), (8, 128))
-
-
-def advance(time_step, state, rate, drag_k, infil, c, r):
+    top = lax.fori_loop(1, ITERS, lambda it, top: before_apply(it, apply(top, it)), top)
+    top_out[...] = jnp.broadcast_to(top, (8, 128))
+
+    for g in range(len(GROUPS)):
+        group_copy(g).wait_send()
+    for it in range(ITERS):
+        for copy in halo_copies(it):
+            copy.wait_send()
+        if it > 0:
+            max_copy(it, 0).wait_send()
+            max_copy(it, 1).wait_send()
+
+
+def advance(time_step, state, rate, drag_k, c, r):
     inner, rows = pl.ds(r * 8, 8), pl.ds(TOP + r * 8, 8)
-    wet = state[0, c + 1, rows, :] + time_step * rate[0, c, inner, :]
-    depth = jnp.maximum(wet - time_step * infil[c, inner, :], 0.0)
+    depth = jnp.maximum(state[0, c + 1, rows, :] + time_step * rate[0, c, inner, :], 0.0)
     slow = inverse_of(1.0 + time_step * drag_k[c, inner, :])
     east = (state[1, c + 1, rows, :] + time_step * rate[1, c, inner, :]) * slow
     north = (state[2, c + 1, rows, :] + time_step * rate[2, c, inner, :]) * slow
     return depth, east, north
 
 
-def last_step(state, rate, drag_k, infil, top, depth_out, east_out, north_out, panels, out_sem):
-    time_step = (COURANT * CELL_SIZE) / top[...]
+def last_step(state, rate, drag_k, top, depth_out, east_out, north_out, panels, out_sem):
+    time_step = (COURANT * CELL_SIZE) * inverse_of(top[...])
     stores = []
-    for c in range(CG):
-        for r in range(8):
-            for f, value in enumerate(advance(time_step, state, rate, drag_k, infil, c, r)):
-                panels[f, c, pl.ds(r * 8, 8), :] = value
+    for r in range(8):
+        rows = pl.ds(r * 8, 8)
+        for c in range(CG):
+            for f, value in enumerate(advance(time_step, state, rate, drag_k, c, r)):
+                panels[f, rows, pl.ds(c * 128, 128)] = value
         for f, out in enumerate((depth_out, east_out, north_out)):
-            copy = pltpu.make_async_copy(panels.at[f, c], out.at[:, pl.ds(c * 128, 128)], out_sem.at[f, c])
+            copy = pltpu.make_async_copy(panels.at[f, rows], out.at[rows], out_sem.at[f, r])
             copy.start()
             stores.append(copy)
     for copy in stores:
@@ -584,12 +610,12 @@
             pltpu.VMEM((3,) + padded, F32),
             pltpu.VMEM((3,) + cells, F32),
             pltpu.VMEM(cells, F32),
-            pltpu.VMEM(cells, F32),
             pltpu.VMEM((8, 128), F32),
         ),
         in_specs=[anywhere] * 12,
-        out_specs=(vmem,) * 5,
+        out_specs=(vmem,) * 4,
         scratch_shapes=[
+            pltpu.VMEM(cells, F32),
             pltpu.SMEM(infil_table.shape, F32),
             pltpu.SMEM(rough_table.shape, F32),
             pltpu.VMEM(reflectance.shape, BF16),
@@ -618,12 +644,12 @@
             pltpu.VMEM((ITERS, 2, 8, 128), F32),
             pltpu.VMEM((ITERS, 2, 8, 128), F32),
             pltpu.SemaphoreType.DMA((7 + 5 * CG,)),
-            pltpu.SemaphoreType.DMA((GROUPS,)),
-            pltpu.SemaphoreType.DMA((GROUPS,)),
+            pltpu.SemaphoreType.DMA((len(GROUPS),)),
+            pltpu.SemaphoreType.DMA((len(GROUPS),)),
             pltpu.SemaphoreType.DMA((ITERS, 4)),
             pltpu.SemaphoreType.DMA((ITERS, 4)),
-            pltpu.SemaphoreType.DMA((ITERS,)),
-            pltpu.SemaphoreType.DMA((ITERS,)),
+            pltpu.SemaphoreType.DMA((ITERS, 2)),
+            pltpu.SemaphoreType.DMA((ITERS, 2)),
         ],
         compiler_params=pltpu.CompilerParams(
             collective_id=0, has_side_effects=True, vmem_limit_bytes=48 * 2**20
@@ -633,9 +659,9 @@
     return pl.pallas_call(
         last_step,
         out_shape=(grid, grid, grid),
-        in_specs=[vmem] * 5,
+        in_specs=[vmem] * 4,
         out_specs=(anywhere,) * 3,
-        scratch_shapes=[pltpu.VMEM((3,) + cells, F32), pltpu.SemaphoreType.DMA((3, CG))],
+        scratch_shapes=[pltpu.VMEM((3,) + depth0.shape, F32), pltpu.SemaphoreType.DMA((3, CG))],
         compiler_params=pltpu.CompilerParams(vmem_limit_bytes=4 * 2**20),
     )(*[pltpu.with_memory_space_constraint(result, pltpu.VMEM) for result in results])
 

time: 55.8 us -> 55.1 us (0.987)
  Pallas kernels: 55.1 us -> 54.3 us
    pallas_call x1, Pallas kernels: 54 us -> 53.2 us  [body(): pl.pallas_call(kernel, out_shape=(pltpu.VMEM((3,) + padded, F32), pltpu.V...]
where the time goes in v3:
time: 55.1 us; the launch traced here: 55 us
  Pallas kernels  54.3 us (99%)
  between operations  0.64 us (1%)
    pallas_call x1, Pallas kernels, body(): pl.pallas_call(kernel, out_shape=(pltpu.VMEM((3,) + padded, F32), pltpu.V...  53.2 us

profile of v3, /device:TPU:1, one launch (start us, length us, event | category | flops | bytes accessed | tf_op | source)
XLA Modules:
  0.0 55.0 jit_solution(6447021523356919813)
XLA Ops:
  0.6 53.2 %shard_map.139 = (f32[3,10,80,128]{3,2,1,0:T(8,128)S(1)}, f32[3,8,64,128]{3,2,1,0:T(8,128)S(1)}, f32[8,64,128]{2,1,0:T(8,128)S(1)}, f32[8,128]{1,0:T(8,128)S(1)}) custom-call(bf16[4,512,128]{2,1,0:T(8,128)(2,1)} %refl_hbm.1, s32[1,512]{1,0:T(1,128)} %bitcast.3, s32[1,512]{1,0:T(1,128)} %bitcast.4, s32[1,512]{1,0:T(1,128)} %bitcast.5, ...), custom_call_target="tpu_custom_call" | custom-call | flops 1000000000 | bytes 3000000 | tf_op jit(solution)/shard_map/pallas_call | solution.py:607
  53.9 1.1 %shard_map.140 = (f32[64,1024]{1,0:T(8,128)}, f32[64,1024]{1,0:T(8,128)}, f32[64,1024]{1,0:T(8,128)}) custom-call(f32[3,10,80,128]{3,2,1,0:T(8,128)S(1)} %get-tuple-element.7.state, f32[3,8,64,128]{3,2,1,0:T(8,128)S(1)} %get-tuple-element.8.rate, f32[8,64,128]{2,1,0:T(8,128)S(1)} %get-tuple-element.9.drag_k, f32[8,128]{1,0:T(8,128)S(1)} %get-tuple-element.10.top), custom_call_target="tpu_custom_call" | custom-call | tf_op jit(solution)/shard_map/pallas_call | solution.py:659

commit v4 on v3

--- a/solution.py
+++ b/solution.py
@@ -27,7 +27,7 @@
         for y in range(4)
         if (x, core, z, y) != (0, 0, 0, 0)
     ],
-    key=lambda o: (-(HOPS[o[0]] + HOPS[o[2]] + HOPS[o[3]]), -o[1]),
+    key=lambda o: (-(HOPS[o[0]] + HOPS[o[2]] + HOPS[o[3]]), o[1]),
 )
 PEERS = len(OFFSETS)
 FAR = 14
@@ -270,10 +270,11 @@
 
     pl.semaphore_wait(barrier, PEERS)
 
-    for copy in halo_copies(0):
-        copy.start()
     for k, o in enumerate(OFFSETS):
         there = target(o)
+        if k == FAR:
+            for copy in halo_copies(0):
+                copy.start()
         pltpu.make_async_remote_copy(
             src_ref=outgoing.at[there],
             dst_ref=incoming.at[k],

time: 55.1 us -> 54.9 us (level)
  no operation moved by 1% of the time
where the time goes in v4:
time: 54.9 us; the launch traced here: 54.8 us
  Pallas kernels  54.1 us (99%)
  between operations  0.64 us (1%)
    pallas_call x1, Pallas kernels, body(): pl.pallas_call(kernel, out_shape=(pltpu.VMEM((3,) + padded, F32), pltpu.V...  53 us
    pallas_call x1, Pallas kernels, body(): pl.pallas_call(last_step, out_shape=(grid, grid, grid), in_specs=[vmem] *...  1.1 us

profile of v4, /device:TPU:1, one launch (start us, length us, event | category | flops | bytes accessed | tf_op | source)
XLA Modules:
  0.0 54.8 jit_solution(18101739229305561602)
XLA Ops:
  0.6 53.0 %shard_map.139 = (f32[3,10,80,128]{3,2,1,0:T(8,128)S(1)}, f32[3,8,64,128]{3,2,1,0:T(8,128)S(1)}, f32[8,64,128]{2,1,0:T(8,128)S(1)}, f32[8,128]{1,0:T(8,128)S(1)}) custom-call(bf16[4,512,128]{2,1,0:T(8,128)(2,1)} %refl_hbm.1, s32[1,512]{1,0:T(1,128)} %bitcast.3, s32[1,512]{1,0:T(1,128)} %bitcast.4, s32[1,512]{1,0:T(1,128)} %bitcast.5, ...), custom_call_target="tpu_custom_call" | custom-call | flops 1000000000 | bytes 3000000 | tf_op jit(solution)/shard_map/pallas_call | solution.py:608
  53.7 1.1 %shard_map.140 = (f32[64,1024]{1,0:T(8,128)}, f32[64,1024]{1,0:T(8,128)}, f32[64,1024]{1,0:T(8,128)}) custom-call(f32[3,10,80,128]{3,2,1,0:T(8,128)S(1)} %get-tuple-element.7.state, f32[3,8,64,128]{3,2,1,0:T(8,128)S(1)} %get-tuple-element.8.rate, f32[8,64,128]{2,1,0:T(8,128)S(1)} %get-tuple-element.9.drag_k, f32[8,128]{1,0:T(8,128)S(1)} %get-tuple-element.10.top), custom_call_target="tpu_custom_call" | custom-call | tf_op jit(solution)/shard_map/pallas_call | solution.py:660
